TPU v7x, 256 devices: a whole 4x4x8 slice. The times are simulated.
256 devices in a mesh: inp: 4 (over z_hi), out: 8 (over y, core), dep: 8 (over z_lo, x).
Axes of the slice: x: 4, y: 4, z: 8 (z_hi: 4, z_lo: 2; z = z_hi * 2 + z_lo), core: 2. Of those that a mesh axis runs over, the one named last changes fastest.
Arguments:
- tokens: bfloat16 [3072, 6144], P(('dep', 'out'), 'inp'), may hold values from -6 to 6
- cotangent: bfloat16 [3072, 6144], P(('dep', 'out'), 'inp'), may hold values from -16 to 16
- weight_in: bfloat16 [6144, 12288], P(('inp', 'dep'), 'out'), may hold values from -0.078125 to 0.078125
- weight_out: bfloat16 [12288, 6144], P(('out', 'dep'), 'inp'), may hold values from -0.0546875 to 0.0546875
Outputs:
- tokens_grad: bfloat16 [3072, 6144], P(('dep', 'out'), 'inp')
- weight_in_grad: bfloat16 [6144, 12288], P(('inp', 'dep'), 'out')
- weight_out_grad: bfloat16 [12288, 6144], P(('out', 'dep'), 'inp')
All inputs are finite; a program needn't handle non-finite values.
Results may differ from a plain program's by a relative error of at most 0.025.
Values may be sent and summed in bfloat16 or wider, within the bound.
A program may use at most 64 MiB of HBM per device.

v0:
```python
import jax
import jax.numpy as jnp
from jax import lax
from jax.sharding import PartitionSpec as P


def gelu_parts(preact):
    normal_cdf = 0.5 * (1.0 + lax.erf(preact * 0.7071067811865476))
    density = jnp.exp(-0.5 * preact * preact) * 0.3989422804014327
    return (preact * normal_cdf, normal_cdf + preact * density)


def hidden_step(preact, act_grad):
    values, slopes = gelu_parts(preact)
    return (values.astype(jnp.bfloat16), (act_grad * slopes).astype(jnp.bfloat16))


def shards(tokens, cotangent, weight_in, weight_out):
    features, grads = (
        lax.all_gather(tokens, "out", axis=0, tiled=True),
        lax.all_gather(cotangent, "out", axis=0, tiled=True),
    )
    token_rows = features.shape[0]
    grad_scale = float(token_rows * lax.axis_size("dep")) ** (-0.5)
    whole_in = lax.all_gather(weight_in, "dep", axis=0, tiled=True)
    preact_part = jnp.dot(features, whole_in, preferred_element_type=jnp.float32)
    act_grad_part = lax.dot_general(
        grads,
        lax.all_gather(weight_out, "dep", axis=0, tiled=True),
        (((1,), (1,)), ((), ())),
        preferred_element_type=jnp.float32,
    )
    preact, act_grad = (
        lax.psum(preact_part.astype(jnp.bfloat16), "inp").astype(jnp.float32),
        lax.psum(act_grad_part.astype(jnp.bfloat16), "inp").astype(jnp.float32),
    )
    hidden_act, pre_grad = hidden_step(preact, act_grad)
    tokens_part = lax.dot_general(
        pre_grad, whole_in, (((1,), (1,)), ((), ())), preferred_element_type=jnp.float32
    )
    tokens_grad = lax.psum_scatter(
        tokens_part.astype(jnp.bfloat16), "out", scatter_dimension=0, tiled=True
    )
    product = lax.dot_general(
        features, pre_grad, (((0,), (0,)), ((), ())), preferred_element_type=jnp.float32
    )
    weight_in_grad = lax.psum_scatter(
        (grad_scale * product).astype(jnp.bfloat16), "dep", scatter_dimension=0, tiled=True
    )
    out_term = grad_scale * lax.dot_general(
        hidden_act, grads, (((0,), (0,)), ((), ())), preferred_element_type=jnp.float32
    )
    weight_out_grad = lax.psum_scatter(
        out_term.astype(jnp.bfloat16), "dep", scatter_dimension=0, tiled=True
    )
    return (tokens_grad, weight_in_grad, weight_out_grad)


def solution(mesh):
    in_specs = (
        P(("dep", "out"), "inp"),
        P(("dep", "out"), "inp"),
        P(("inp", "dep"), "out"),
        P(("out", "dep"), "inp"),
    )
    out_specs = (P(("dep", "out"), "inp"), P(("inp", "dep"), "out"), P(("out", "dep"), "inp"))
    return jax.shard_map(shards, mesh=mesh, in_specs=in_specs, out_specs=out_specs, check_vma=False)
```

profile of v0, /device:TPU:2, one launch (start us, length us, event | category | flops | bytes accessed | tf_op | source)
XLA Modules:
  0.0 473.4 jit_solution(7504695294582602302)
XLA Ops:
  7.2 0.7 all-gather.5.cloned.1.call-update
  7.9 0.7 all-gather.7.cloned.1.call-update
  8.7 0.7 all-gather.9.cloned.1.call-update
  9.4 0.5 all-gather.11.cloned.1.call-update
  10.0 29.0 %all-gather.5.cloned.1.call-done = bf16[384,1536]{1,0:T(8,128)(2,1)} async-done(((bf16[48,1536]{1,0:T(8,128)(2,1)}), bf16[384,1536]{1,0:T(8,128)(2,1)}) %all-gather.5.cloned.1.call-update) | async-done | bytes 1179664 | tf_op jit(solution)/shard_map/all_gather | solution.py:21
  39.0 59.8 %all-gather.7.cloned.1.call-done = bf16[1536,1536]{1,0:T(8,128)(2,1)} async-done(((bf16[192,1536]{1,0:T(8,128)(2,1)}), bf16[1536,1536]{1,0:T(8,128)(2,1)}) %all-gather.7.cloned.1.call-update) | async-done | bytes 4718608 | tf_op jit(solution)/shard_map/all_gather | solution.py:29
  98.8 5.7 %convolution_convert_fusion.2 = bf16[384,1536]{1,0:T(8,128)(2,1)} fusion(bf16[384,1536]{1,0:T(8,128)(2,1)} %all-gather.5.cloned.1.call-done, bf16[1536,1536]{1,0:T(8,128)(2,1)} %all-gather.7.cloned.1.call-done), kind=kOutput, calls=%fused_computation.12 | convolution fusion | flops 1812529152 | bytes 7077888 | tf_op jit(solution)/shard_map/dot_general | solution.py:27
  104.5 23.3 %all-gather.9.cloned.1.call-done = bf16[384,1536]{1,0:T(8,128)(2,1)} async-done(((bf16[48,1536]{1,0:T(8,128)(2,1)}), bf16[384,1536]{1,0:T(8,128)(2,1)}) %all-gather.9.cloned.1.call-update) | async-done | bytes 1179664 | tf_op jit(solution)/shard_map/all_gather | solution.py:20
  127.8 59.6 %all-gather.11.cloned.1.call-done = bf16[1536,1536]{1,0:T(8,128)(2,1)} async-done(((bf16[192,1536]{1,0:T(8,128)(2,1)}), bf16[1536,1536]{1,0:T(8,128)(2,1)}) %all-gather.11.cloned.1.call-update) | async-done | bytes 4718608 | tf_op jit(solution)/shard_map/all_gather | solution.py:25
  187.5 5.7 %convolution_convert_fusion.1 = bf16[384,1536]{1,0:T(8,128)(2,1)} fusion(bf16[384,1536]{1,0:T(8,128)(2,1)} %all-gather.9.cloned.1.call-done, bf16[1536,1536]{1,0:T(8,128)(2,1)} %all-gather.11.cloned.1.call-done), kind=kOutput, calls=%fused_computation.11 | convolution fusion | flops 1812529152 | bytes 7077888 | tf_op jit(solution)/shard_map/dot_general | solution.py:26
  193.2 0.0 reduce-scatter.6.cloned.1.call-start
  193.3 109.4 %all-reduce.3.cloned.1.call-done = (bf16[384,1536]{1,0:T(8,128)(2,1)}, bf16[384,1536]{1,0:T(8,128)(2,1)}) async-done(((bf16[384,1536]{1,0:T(8,128)(2,1)}, bf16[384,1536]{1,0:T(8,128)(2,1)}), (bf16[384,1536]{1,0:T(8,128)(2,1)}, bf16[384,1536]{1,0:T(8,128)(2,1)})) %all-reduce.3.cloned.1.call-update) | async-done | bytes 2359312 | tf_op jit(solution)/shard_map/psum | solution.py:34
  302.7 2.4 fusion.10
  305.1 5.5 %convolution_convert_fusion = bf16[384,1536]{1,0:T(8,128)(2,1)} fusion(bf16[384,1536]{1,0:T(8,128)(2,1)S(1)} %fusion.10, bf16[1536,1536]{1,0:T(8,128)(2,1)} %all-gather.11.cloned.1.call-done), kind=kOutput, calls=%fused_computation.10 | convolution fusion | flops 1812529152 | bytes 7077888 | tf_op jit(solution)/shard_map/dot_general | solution.py:38
  310.6 0.0 reduce-scatter.10.cloned.1.call-start
  310.7 4.4 fusion.2
  315.1 6.7 %copy.9 = bf16[1536,1536]{1,0:T(8,128)(2,1)} copy(bf16[1536,1536]{0,1:T(8,128)(2,1)} %fusion.2) | data formatting | bytes 9437184
  321.8 0.0 reduce-scatter.8.cloned.1.call-start
  321.9 1.2 copy-done
  323.1 0.4 copy-done.1
  323.4 4.4 fusion.1
  327.8 15.9 %reduce-scatter.6.cloned.1.call-done = bf16[48,1536]{1,0:T(8,128)(2,1)} async-done(((bf16[384,1536]{1,0:T(8,128)(2,1)}), bf16[48,1536]{1,0:T(8,128)(2,1)}) %reduce-scatter.6.cloned.1.call-update) | async-done | bytes 147472 | tf_op jit(solution)/shard_map/reduce_scatter | solution.py:41
  343.7 60.3 %reduce-scatter.10.cloned.1.call-done = bf16[192,1536]{1,0:T(8,128)(2,1)} async-done(((bf16[1536,1536]{1,0:T(8,128)(2,1)}), bf16[192,1536]{1,0:T(8,128)(2,1)}) %reduce-scatter.10.cloned.1.call-update) | async-done | bytes 589840
  404.0 62.6 %reduce-scatter.8.cloned.1.call-done = bf16[192,1536]{1,0:T(8,128)(2,1)} async-done(((bf16[1536,1536]{1,0:T(8,128)(2,1)}), bf16[192,1536]{1,0:T(8,128)(2,1)}) %reduce-scatter.8.cloned.1.call-update) | async-done | bytes 589840 | tf_op jit(solution)/shard_map/reduce_scatter | solution.py:53
  (13 shorter events, 0.3 us)
Async XLA Ops:
  7.2 31.9 %all-gather.5.cloned.1.call-start = ((), (), s32[]{:S(2)}) async-start(), calls=%async_computation.3 | async-start | bytes 1327104 | tf_op jit(solution)/shard_map/all_gather | solution.py:21
  7.9 90.9 %all-gather.7.cloned.1.call-start = ((), (), s32[]{:S(2)}) async-start(), calls=%async_computation.4 | async-start | bytes 5308416 | tf_op jit(solution)/shard_map/all_gather | solution.py:29
  8.6 119.2 %all-gather.9.cloned.1.call-start = ((), (), s32[]{:S(2)}) async-start(), calls=%async_computation.5 | async-start | bytes 1327104 | tf_op jit(solution)/shard_map/all_gather | solution.py:20
  9.4 178.1 %all-gather.11.cloned.1.call-start = ((), (), s32[]{:S(2)}) async-start(), calls=%async_computation.6 | async-start | bytes 5308416 | tf_op jit(solution)/shard_map/all_gather | solution.py:25
  10.0 292.8 %all-reduce.3.cloned.1.call-start = ((), (), s32[]{:S(2)}) async-start(), calls=%async_computation.10 | async-start | bytes 4718592 | tf_op jit(solution)/shard_map/psum | solution.py:34
  193.2 150.5 %reduce-scatter.6.cloned.1.call-start = ((), (), s32[]{:S(2)}) async-start(), calls=%async_computation.7 | async-start | bytes 1327104 | tf_op jit(solution)/shard_map/reduce_scatter | solution.py:41
  305.1 5.6 %copy-start.2 = (bf16[384,1536]{1,0:T(8,128)(2,1)S(1)}, bf16[384,1536]{1,0:T(8,128)(2,1)}, u32[]{:S(2)}) copy-start(bf16[384,1536]{1,0:T(8,128)(2,1)} %all-gather.9.cloned.1.call-done) | copy-start | bytes 3538948
  310.6 93.4 %reduce-scatter.10.cloned.1.call-start = ((), (), s32[]{:S(2)}) async-start(), calls=%async_computation.9 | async-start | bytes 5308416
  321.8 1.3 copy-start
  321.8 1.6 copy-start.1
  321.8 144.7 %reduce-scatter.8.cloned.1.call-start = ((), (), s32[]{:S(2)}) async-start(), calls=%async_computation.8 | async-start | bytes 5308416 | tf_op jit(solution)/shard_map/reduce_scatter | solution.py:53
Sparse Core Ops, SparseCore 0:
  9.8 29.1 all-gather.4
  40.8 57.9 all-gather.6
  100.6 27.1 all-gather.8
  129.5 57.9 all-gather.10
  193.3 109.3 all-reduce.2
  310.7 32.9 reduce-scatter.5
  346.8 57.1 reduce-scatter.9
  407.1 59.3 reduce-scatter.7
where the time goes:
time: 477 us; the launch traced here: 473 us
  waiting for transfers between devices  423 us (89%)
  matrix products  25.8 us (5%)
  between operations  14.2 us (3%)
  local copies, waits for them, and re-layouts  8.24 us (2%)
    psum x1, waiting for transfers between devices, shards(): lax.psum(preact_part.astype(jnp.bfloat16), 'inp').astype(jnp.float32)  109 us
    unnamed x9, waiting for transfers between devices  63 us
    reduce_scatter x1, waiting for transfers between devices, shards(): lax.psum_scatter(out_term.astype(jnp.bfloat16), 'dep', scatter_dimension=...  62.6 us
    all_gather x1, waiting for transfers between devices, shards(): lax.all_gather(weight_out, 'dep', axis=0, tiled=True)  59.8 us
    all_gather x1, waiting for transfers between devices, shards(): whole_in = lax.all_gather(weight_in, 'dep', axis=0, tiled=True)  59.6 us
    all_gather x1, waiting for transfers between devices, shards(): lax.all_gather(cotangent, 'out', axis=0, tiled=True)  29 us
    all_gather x1, waiting for transfers between devices, shards(): lax.all_gather(tokens, 'out', axis=0, tiled=True)  23.3 us
    reduce_scatter x1, waiting for transfers between devices, shards(): lax.psum_scatter(tokens_part.astype(jnp.bfloat16), 'out', scatter_dimensi...  15.9 us
  transfers between devices with their start and end apart: 8, of which 8 were waited for; matrix products, arithmetic and copies ran while one was open for 4% of the time, Pallas kernels for 0%

commit v1 on v0

v1 whole, which is shorter than its diff:
```python
import functools

import jax
import jax.numpy as jnp
from jax import lax
from jax.experimental import pallas as pl
from jax.experimental.pallas import tpu as pltpu
from jax.sharding import PartitionSpec as P

MESH = pl.DeviceIdType.MESH
BF16, F32 = jnp.bfloat16, jnp.float32
NJ, CH = 3, 256
ND, DC = 3, 512
TB, WB = 48, 192
TOK, WID, HID = 768, 1536, 768
OWN = 192


def dot(a, b, ca, cb):
    return lax.dot_general(a, b, (((ca,), (cb,)), ((), ())), preferred_element_type=F32)


def gelu_parts(preact):
    normal_cdf = 0.5 * (1.0 + lax.erf(preact * 0.7071067811865476))
    density = jnp.exp(-0.5 * preact * preact) * 0.3989422804014327
    return preact * normal_cdf, normal_cdf + preact * density


def kernel(
    scale, tok, cot, win, wout, o_tok, o_win, o_wout,
    tg, wi, wo, pf, ps, pr, hg, slope, dwof, dwos, dwor, dwif, dwis, dwir, dwcs, dwcr,
    dxf, dxss, dxsr, dxyf, dxys, dxyr, dxcs, dxcr,
    m_loc, m_agc, m_agy, m_ags, m_wic, m_wix, m_wox, m_rs, m_hg, m_dwo, m_dwi, m_dwc, m_dxs, m_dxy, m_dxc,
):
    k, out, dep = lax.axis_index("inp"), lax.axis_index("out"), lax.axis_index("dep")
    y, co, c, x = out // 2, out % 2, dep // 4, dep % 4
    oc, oco = 1 - c, 1 - co

    def dev(dk=0, dy=0, dx=0, fc=0, fs=0):
        o = (y + dy) % 4 * 2 + (oco if fs else co)
        d = (oc if fc else c) * 4 + (x + dx) % 4
        return {"inp": (k + dk) % 4, "out": o, "dep": d}

    def cp(src, dst, sem, idx, to):
        return pltpu.make_async_remote_copy(
            src_ref=src, dst_ref=dst, send_sem=sem.at[(0,) + idx], recv_sem=sem.at[(1,) + idx],
            device_id=to, device_id_type=MESH,
        )

    def rows(start, n):
        return pl.ds(pl.multiple_of(start, 16), n)

    def tslot(a, cc, yy, oo):
        return tg.at[a, rows(((cc * 4 + yy) * 2 + oo) * TB, TB)]

    def ag_c(a):
        return cp((tok, cot)[a], tslot(a, c, y, co), m_agc, (a,), dev(fc=1))

    def ag_y(a, p, dy):
        slot = tslot(a, oc if p else c, y, co)
        return cp(slot if p else (tok, cot)[a], slot, m_agy, (a, p, dy - 1), dev(dy=dy))

    def ag_s(a, p, dy):
        slot = tslot(a, oc if p else c, (y + 4 - dy) % 4, co)
        src = (tok, cot)[a] if (p == 0 and dy == 0) else slot
        return cp(src, slot, m_ags, (a, p, dy), dev(fs=1))

    def wslot(j, cc, xx):
        return wi.at[j, rows((cc * 4 + xx) * WB, WB)]

    def wcols(cc, j):
        return win.at[:, pl.ds(pl.multiple_of(cc * HID + j * CH, CH), CH)]

    def wi_c(j):
        return cp(wcols(oc, j), wslot(j, c, x), m_wic, (j,), dev(fc=1))

    def wi_x(j, p, dx):
        slot = wslot(j, oc if p else c, x)
        return cp(slot if p else wcols(c, j), slot, m_wix, (j, p, dx - 1), dev(dx=dx))

    def wo_x(dx):
        return cp(wout, wo.at[rows(x * WB, WB)], m_wox, (dx - 1,), dev(dx=dx))

    def rs(a, j, dz):
        return cp(ps.at[a, j, rows((k + dz) % 4 * OWN, OWN)], pr.at[a, j, dz - 1], m_rs, (a, j, dz - 1), dev(dk=dz))

    def ag_h(a, j, dz):
        slot = hg.at[a, j, rows(k * OWN, OWN)]
        return cp(slot, slot, m_hg, (a, j, dz - 1), dev(dk=dz))

    def dwo_x(dx):
        return cp(dwos.at[rows((x + dx) % 4 * WB, WB)], dwor.at[dx - 1], m_dwo, (dx - 1,), dev(dx=dx))

    def dwi_x(j, cc, dx):
        src = dwis.at[j, rows((cc * 4 + (x + dx) % 4) * WB, WB)]
        return cp(src, dwir.at[j, dx - 1, cc], m_dwi, (j, dx - 1, cc), dev(dx=dx))

    def dw_c(j):
        return cp(dwcs.at[j], dwcr.at[j], m_dwc, (j,), dev(fc=1))

    def dx_s(d):
        return cp(dxss.at[d], dxsr.at[d], m_dxs, (d,), dev(fs=1))

    def dx_y(d, dy):
        return cp(dxys.at[d, (y + dy) % 4], dxyr.at[d, dy - 1], m_dxy, (d, dy - 1), dev(dy=dy))

    def dx_c(d):
        return cp(dxcs.at[d], dxcr.at[d], m_dxc, (d,), dev(fc=1))

    local = [pltpu.make_async_copy((tok, cot)[a], tslot(a, c, y, co), m_loc.at[a]) for a in range(2)]
    local += [pltpu.make_async_copy(wcols(c, j), wslot(j, c, x), m_loc.at[2 + j]) for j in range(NJ)]
    local += [pltpu.make_async_copy(wout, wo.at[rows(x * WB, WB)], m_loc.at[5])]
    for copy in local:
        copy.start()
    barrier = pltpu.get_barrier_semaphore()
    partners = [dev(fs=1), dev(fc=1)]
    for d in (1, 2, 3):
        partners += [dev(dk=d), dev(dy=d), dev(dx=d)]
    for to in partners:
        pl.semaphore_signal(barrier, inc=1, device_id=to, device_id_type=MESH)
    pl.semaphore_wait(barrier, len(partners))

    wi_c(0).start()
    for d in (2, 1, 3):
        wi_x(0, 0, d).start()
        ag_y(0, 0, d).start()
    ag_c(0).start()
    ag_s(0, 0, 0).start()
    wi_c(1).start()
    wi_c(2).start()
    ag_c(1).start()
    wi_c(0).wait_recv()
    for d in (2, 1, 3):
        wi_x(0, 1, d).start()
    ag_c(0).wait_recv()
    for d in (2, 1, 3):
        ag_y(0, 1, d).start()
    ag_s(0, 1, 0).start()
    for j in (1, 2):
        for d in (2, 1, 3):
            wi_x(j, 0, d).start()
        wi_c(j).wait_recv()
        for d in (2, 1, 3):
            wi_x(j, 1, d).start()
    for d in (2, 1, 3):
        wo_x(d).start()
    for p in (0, 1):
        for d in (1, 3, 2):
            ag_y(0, p, d).wait_recv()
            ag_s(0, p, d).start()
    for d in (2, 1, 3):
        ag_y(1, 0, d).start()
    ag_s(1, 0, 0).start()
    ag_c(1).wait_recv()
    for d in (2, 1, 3):
        ag_y(1, 1, d).start()
    ag_s(1, 1, 0).start()
    for copy in local:
        copy.wait()
    for p in (0, 1):
        for d in range(4):
            ag_s(0, p, d).wait_recv()

    def product(a, j, value):
        pf[a, j] = value
        ps[a, j] = value.astype(BF16)
        for d in (2, 1, 3):
            rs(a, j, d).start()

    def total(a, j):
        for d in (1, 2, 3):
            rs(a, j, d).wait_recv()
        value = pf[a, j, rows(k * OWN, OWN)]
        for d in range(3):
            value = value + pr[a, j, d].astype(F32)
        return value

    def share(a, j, value):
        hg[a, j, rows(k * OWN, OWN)] = value.astype(BF16)
        for d in (2, 1, 3):
            ag_h(a, j, d).start()

    @pl.loop(0, NJ)
    def _(j):
        for p in (0, 1):
            for d in (1, 2, 3):
                wi_x(j, p, d).wait_recv()
        product(0, j, dot(tg[0], wi[j], 1, 0))

    for p in (0, 1):
        for d in (1, 3, 2):
            ag_y(1, p, d).wait_recv()
            ag_s(1, p, d).start()

    @pl.loop(0, NJ)
    def _(j):
        value, slope_j = gelu_parts(total(0, j))
        slope[j] = slope_j
        share(0, j, value)

    for p in (0, 1):
        for d in range(4):
            ag_s(1, p, d).wait_recv()
    for d in (1, 2, 3):
        wo_x(d).wait_recv()

    @pl.loop(0, NJ)
    def _(j):
        product(1, j, dot(tg[1], wo[rows(j * CH, CH)], 1, 1))

    @pl.loop(0, NJ)
    def _(j):
        for d in (1, 2, 3):
            ag_h(0, j, d).wait_recv()
        value = scale * dot(hg[0, j], tg[1], 0, 0)
        dwof[rows(j * CH, CH)] = value
        dwos[rows(j * CH, CH)] = value.astype(BF16)

    for d in (2, 1, 3):
        dwo_x(d).start()

    @pl.loop(0, NJ)
    def _(j):
        share(1, j, total(1, j) * slope[j])

    def weight_in_part(j):
        value = scale * dot(tg[0], hg[1, j], 0, 0)
        dwif[j] = value
        dwis[j] = value.astype(BF16)
        for d in (2, 1, 3):
            for cc in range(2):
                dwi_x(j, cc, d).start()

    def cols(d):
        return pl.ds(pl.multiple_of(d * DC, DC), DC)

    @pl.loop(0, NJ - 1)
    def _(j):
        for d in (1, 2, 3):
            ag_h(1, j, d).wait_recv()
        weight_in_part(j)

        @pl.loop(0, ND)
        def _(d):
            part = dot(hg[1, j], wi[j, cols(d)], 1, 1)

            @pl.when(j == 0)
            def _():
                dxf[d] = part

            @pl.when(j > 0)
            def _():
                dxf[d] += part

    for d in (1, 2, 3):
        dwo_x(d).wait_recv()
    value = dwof[rows(x * WB, WB)]
    for d in range(3):
        value = value + dwor[d].astype(F32)
    o_wout[...] = value.astype(BF16)

    for d in (1, 2, 3):
        ag_h(1, NJ - 1, d).wait_recv()

    @pl.loop(0, ND)
    def _(d):
        dxf[d] += dot(hg[1, NJ - 1], wi[NJ - 1, cols(d)], 1, 1)
        for b in range(8):
            dxss[d, b] = dxf[d, rows((b * 2 + oco) * TB, TB)].astype(BF16)
        dx_s(d).start()

    weight_in_part(NJ - 1)

    @pl.loop(0, ND)
    def _(d):
        dx_s(d).wait_recv()
        for cc in range(2):
            for yy in range(4):
                b = cc * 4 + yy
                part = dxf[d, rows((b * 2 + co) * TB, TB)] + dxsr[d, b].astype(F32)
                dxyf[d, yy, cc] = part
                dxys[d, yy, cc] = part.astype(BF16)
        for dy in (2, 1, 3):
            dx_y(d, dy).start()

    def weight_in_send(j):
        for d in (1, 2, 3):
            for cc in range(2):
                dwi_x(j, cc, d).wait_recv()
        value = dwif[j, rows((oc * 4 + x) * WB, WB)]
        for d in range(3):
            value = value + dwir[j, d, oc].astype(F32)
        dwcs[j] = value.astype(BF16)
        dw_c(j).start()
        value = dwif[j, rows((c * 4 + x) * WB, WB)]
        for d in range(3):
            value = value + dwir[j, d, c].astype(F32)
        o_win[:, pl.ds(pl.multiple_of(c * HID + j * CH, CH), CH)] = value.astype(BF16)

    @pl.loop(0, NJ - 1)
    def _(j):
        weight_in_send(j)

    @pl.loop(0, ND)
    def _(d):
        for dy in (1, 2, 3):
            dx_y(d, dy).wait_recv()
        value = dxyf[d, y, oc]
        for i in range(3):
            value = value + dxyr[d, i, oc].astype(F32)
        dxcs[d] = value.astype(BF16)
        dx_c(d).start()
        value = dxyf[d, y, c]
        for i in range(3):
            value = value + dxyr[d, i, c].astype(F32)
        dxyf[d, y, c] = value

    weight_in_send(NJ - 1)

    @pl.loop(0, ND)
    def _(d):
        dx_c(d).wait_recv()
        o_tok[:, cols(d)] = (dxyf[d, y, c] + dxcr[d].astype(F32)).astype(BF16)

    @pl.loop(0, NJ)
    def _(j):
        dw_c(j).wait_recv()
        o_win[:, pl.ds(pl.multiple_of(oc * HID + j * CH, CH), CH)] = dwcr[j]

    for a in range(2):
        ag_c(a).wait_send()
        for p in range(2):
            for d in (1, 2, 3):
                ag_y(a, p, d).wait_send()
            for d in range(4):
                ag_s(a, p, d).wait_send()
    for d in (1, 2, 3):
        wo_x(d).wait_send()
        dwo_x(d).wait_send()

    @pl.loop(0, NJ)
    def _(j):
        wi_c(j).wait_send()
        dw_c(j).wait_send()
        for d in (1, 2, 3):
            for p in range(2):
                wi_x(j, p, d).wait_send()
                dwi_x(j, p, d).wait_send()
                rs(p, j, d).wait_send()
                ag_h(p, j, d).wait_send()

    @pl.loop(0, ND)
    def _(d):
        dx_s(d).wait_send()
        dx_c(d).wait_send()
        for dy in (1, 2, 3):
            dx_y(d, dy).wait_send()


def shards(tokens, cotangent, weight_in, weight_out):
    scale = float(tokens.shape[0] * lax.axis_size("out") * lax.axis_size("dep")) ** (-0.5)
    vmem, dma = pltpu.VMEM, pltpu.SemaphoreType.DMA
    hbm = pl.BlockSpec(memory_space=pl.ANY)
    own = pl.BlockSpec(memory_space=pltpu.VMEM)
    return pl.pallas_call(
        functools.partial(kernel, scale),
        out_shape=tuple(jax.ShapeDtypeStruct(a.shape, BF16) for a in (tokens, weight_in, weight_out)),
        in_specs=[hbm] * 4,
        out_specs=(own,) * 3,
        scratch_shapes=[
            vmem((2, TOK, WID), BF16),
            vmem((NJ, WID, CH), BF16),
            vmem((HID, WID), BF16),
            vmem((2, NJ, TOK, CH), F32),
            vmem((2, NJ, TOK, CH), BF16),
            vmem((2, NJ, 3, OWN, CH), BF16),
            vmem((2, NJ, TOK, CH), BF16),
            vmem((NJ, OWN, CH), F32),
            vmem((HID, WID), F32),
            vmem((HID, WID), BF16),
            vmem((3, WB, WID), BF16),
            vmem((NJ, WID, CH), F32),
            vmem((NJ, WID, CH), BF16),
            vmem((NJ, 3, 2, WB, CH), BF16),
            vmem((NJ, WB, CH), BF16),
            vmem((NJ, WB, CH), BF16),
            vmem((ND, TOK, DC), F32),
            vmem((ND, 8, TB, DC), BF16),
            vmem((ND, 8, TB, DC), BF16),
            vmem((ND, 4, 2, TB, DC), F32),
            vmem((ND, 4, 2, TB, DC), BF16),
            vmem((ND, 3, 2, TB, DC), BF16),
            vmem((ND, TB, DC), BF16),
            vmem((ND, TB, DC), BF16),
            dma((6,)),
            dma((2, 2)),
            dma((2, 2, 2, 3)),
            dma((2, 2, 2, 4)),
            dma((2, NJ)),
            dma((2, NJ, 2, 3)),
            dma((2, 3)),
            dma((2, 2, NJ, 3)),
            dma((2, 2, NJ, 3)),
            dma((2, 3)),
            dma((2, NJ, 3, 2)),
            dma((2, NJ)),
            dma((2, ND)),
            dma((2, ND, 3)),
            dma((2, ND)),
        ],
        compiler_params=pltpu.CompilerParams(
            collective_id=0, has_side_effects=True, vmem_limit_bytes=61 * 2**20
        ),
        cost_estimate=pl.CostEstimate(flops=11 * 10**9, bytes_accessed=3 * 10**6, transcendentals=0),
    )(tokens, cotangent, weight_in, weight_out)


def solution(mesh):
    in_specs = (
        P(("dep", "out"), "inp"),
        P(("dep", "out"), "inp"),
        P(("inp", "dep"), "out"),
        P(("out", "dep"), "inp"),
    )
    out_specs = (P(("dep", "out"), "inp"), P(("inp", "dep"), "out"), P(("out", "dep"), "inp"))
    return jax.shard_map(shards, mesh=mesh, in_specs=in_specs, out_specs=out_specs, check_vma=False)
```

time: 477 us -> 195 us (0.41)
  waiting for transfers between devices: 423 us -> 0 us
  Pallas kernels: 0 us -> 188 us
  matrix products: 25.8 us -> 0 us
  between operations: 14.2 us -> 0.64 us
    pallas_call x0 -> x1, Pallas kernels: none -> 188 us  [shards(): pl.pallas_call(functools.partial(kernel, scale), out_shape=tuple((jax.Sha...]
    all_gather x4 -> x0, waiting for transfers between devices: 172 us -> none  [the longest x1 59.8 us: shards(): lax.all_gather(weight_out, 'dep', axis=0, tiled=True)]
    psum x1 -> x0, waiting for transfers between devices: 109 us -> none  [shards(): lax.psum(preact_part.astype(jnp.bfloat16), 'inp').astype(jnp.float32)]
    reduce_scatter x2 -> x0, waiting for transfers between devices: 78.4 us -> none  [the longest x1 62.6 us: shards(): lax.psum_scatter(out_term.astype(jnp.bfloat16), 'dep', scatter_dimension=...]
    unnamed x9 -> x0, waiting for transfers between devices: 63 us -> none
    dot_general x5 -> x0, matrix products: 25.8 us -> none  [the longest x1 5.74 us: shards(): lax.dot_general(grads, lax.all_gather(weight_out, 'dep', axis=0, tiled=Tr...]
  transfers between devices with their start and end apart: 8 -> 0, of which waited for: 8 -> 0; matrix products, arithmetic and copies ran while one was open for 4% -> 0% of each run, Pallas kernels for 0% -> 0%
where the time goes in v1:
time: 195 us; the launch traced here: 193 us
  Pallas kernels  188 us (96%)
  local copies, waits for them, and re-layouts  4.38 us (2%)
    pallas_call x1, Pallas kernels, shards(): pl.pallas_call(functools.partial(kernel, scale), out_shape=tuple((jax.Sha...  188 us
    unnamed x5, local copies, waits for them, and re-layouts  4.38 us

profile of v1, /device:TPU:2, one launch (start us, length us, event | category | flops | bytes accessed | tf_op | source)
XLA Modules:
  0.0 193.4 jit_solution(10779467088369820954)
XLA Ops:
  0.6 188.4 %shard_map.67 = (bf16[48,1536]{1,0:T(8,128)(2,1)}, bf16[192,1536]{1,0:T(8,128)(2,1)}, bf16[192,1536]{1,0:T(8,128)(2,1)}) custom-call(bf16[48,1536]{1,0:T(8,128)(2,1)} %tok.1, bf16[48,1536]{1,0:T(8,128)(2,1)} %cot.1, bf16[192,1536]{1,0:T(8,128)(2,1)} %win.1, bf16[192,1536]{1,0:T(8,128)(2,1)} %wout.1), custom_call_target="tpu_custom_call" | custom-call | flops 11000000512 | bytes 3000000 | tf_op jit(solution)/shard_map/pallas_call | solution.py:365
  189.0 1.6 copy.10
  190.6 0.0 copy-start
  190.6 2.0 %copy.11 = bf16[192,1536]{1,0:T(8,128)(2,1)} copy(bf16[192,1536]{1,0:T(8,128)(2,1)} %get-tuple-element.7) | data formatting | bytes 1179648
  192.6 0.0 copy-done
  192.6 0.8 copy.12
Async XLA Ops:
  190.6 2.0 %copy-start = (bf16[192,1536]{1,0:T(8,128)(2,1)S(1)}, bf16[192,1536]{1,0:T(8,128)(2,1)}, u32[]{:S(2)}) copy-start(bf16[192,1536]{1,0:T(8,128)(2,1)} %get-tuple-element.8) | copy-start | bytes 1769476

commit v2 on v0

v2 whole, which is shorter than its diff:
```python
import functools

import jax
import jax.numpy as jnp
from jax import lax
from jax.experimental import pallas as pl
from jax.experimental.pallas import tpu as pltpu
from jax.sharding import PartitionSpec as P

MESH = pl.DeviceIdType.MESH
BF16, F32 = jnp.bfloat16, jnp.float32
NJ, CH = 3, 256
NU = 2 * NJ
ND, DC = 2, 768
TB, WB = 48, 192
TOK, WID, HID = 768, 1536, 768
HALF, OWN = 384, 96


def dot(a, b, ca, cb):
    return lax.dot_general(a, b, (((ca,), (cb,)), ((), ())), preferred_element_type=F32)


def gelu_parts(preact):
    normal_cdf = 0.5 * (1.0 + lax.erf(preact * 0.7071067811865476))
    density = jnp.exp(-0.5 * preact * preact) * 0.3989422804014327
    return preact * normal_cdf, normal_cdf + preact * density


def kernel(
    scale, tok, cot, win, wout, o_tok, o_win, o_wout,
    tg, wi, wo, pf, s1s, s1r, s2s, s2r, hg, slope, dwof, dwos, dwor, dwif, dwis, dwir, dwcs, dwcr,
    dxf, dxss, dxsr, dxyf, dxys, dxyr, dxcs, dxcr,
    m_loc, sent, m_agc, m_agy, m_ags, m_wic, m_wix, m_wox, m_s1, m_s2, m_h1, m_h2, m_dwo, m_dwi, m_dwc, m_dxs, m_dxy, m_dxc,
):
    k, out, dep = lax.axis_index("inp"), lax.axis_index("out"), lax.axis_index("dep")
    y, co, c, x = out // 2, out % 2, dep // 4, dep % 4
    oc, oco = 1 - c, 1 - co
    half = (c, oc)

    def dev(dk=0, dy=0, dx=0, fc=0, fs=0):
        o = (y + dy) % 4 * 2 + (oco if fs else co)
        d = (oc if fc else c) * 4 + (x + dx) % 4
        return {"inp": (k + dk) % 4, "out": o, "dep": d}

    def cp(src, dst, family, recv, to):
        return pltpu.make_async_remote_copy(
            src_ref=src, dst_ref=dst, send_sem=sent.at[family], recv_sem=recv, device_id=to, device_id_type=MESH
        )

    def rows(start, n):
        return pl.ds(pl.multiple_of(start, 16), n)

    def tslot(a, cc, yy, oo):
        return tg.at[a, rows(((cc * 4 + yy) * 2 + oo) * TB, TB)]

    def ag_c(a):
        return cp((tok, cot)[a], tslot(a, c, y, co), 0, m_agc.at[a], dev(fc=1))

    def ag_y(a, p, dy):
        slot = tslot(a, half[p], y, co)
        return cp(slot if p else (tok, cot)[a], slot, 0, m_agy.at[a, p, dy - 1], dev(dy=dy))

    def ag_s(a, p, dy):
        slot = tslot(a, half[p], (y + 4 - dy) % 4, co)
        src = (tok, cot)[a] if (p == 0 and dy == 0) else slot
        return cp(src, slot, 0, m_ags.at[a, p], dev(fs=1))

    def ag_s_all(a, p):
        ref = tg.at[a, pl.ds(0, 4 * TB)]
        return cp(ref, ref, 0, m_ags.at[a, p], dev(fs=1))

    def wslot(j, cc, xx):
        return wi.at[j, rows((cc * 4 + xx) * WB, WB)]

    def wcols(cc, j):
        return win.at[:, pl.ds(pl.multiple_of(cc * HID + j * CH, CH), CH)]

    def wi_c(j):
        return cp(wcols(oc, j), wslot(j, c, x), 1, m_wic.at[j], dev(fc=1))

    def wi_x(j, p, dx):
        slot = wslot(j, half[p], x)
        return cp(slot if p else wcols(c, j), slot, 1, m_wix.at[j], dev(dx=dx))

    def wi_x_all(j):
        ref = wi.at[j, pl.ds(0, 6 * WB)]
        return cp(ref, ref, 1, m_wix.at[j], dev(dx=1))

    def wo_x(dx):
        return cp(wout, wo.at[rows(x * WB, WB)], 2, m_wox, dev(dx=dx))

    def wo_x_all():
        ref = wo.at[pl.ds(0, 3 * WB)]
        return cp(ref, ref, 2, m_wox, dev(dx=1))

    def unit(u):
        i = u % 6
        return (0, i // 2, i % 2) if u < 6 else (1, i % 3, 1 - i // 3)

    def s1(u, r):
        return cp(s1s.at[u, r], s1r.at[u, r], 3, m_s1.at[u, r], dev(dk=(1, 3)[r]))

    def s2(u, r):
        return cp(s2s.at[u, r], s2r.at[u, r], 4, m_s2.at[u, r], dev(dk=(1, 3)[r]))

    def hrows(u, owner, part, n):
        a, j, p = unit(u)
        return hg.at[a, j, rows(half[p] * HALF + owner % 4 * OWN + part * TB, n)]

    def h1(u, r):
        slot = hrows(u, k, 0, OWN)
        return cp(slot, slot, 5, m_h1.at[u, r], dev(dk=(1, 3)[r]))

    def h2(u, r):
        slot = hrows(u, k + (3, 1)[r], r, TB)
        return cp(slot, slot, 5, m_h2.at[u, r], dev(dk=(1, 3)[r]))

    def dwo_x(dx):
        return cp(dwos.at[rows((x + dx) % 4 * WB, WB)], dwor.at[dx - 1], 6, m_dwo, dev(dx=dx))

    def dwo_x_all():
        return cp(dwor, dwor, 6, m_dwo, dev(dx=1))

    def dwi_x(j, p, dx):
        src = dwis.at[j, rows((half[p] * 4 + (x + dx) % 4) * WB, WB)]
        return cp(src, dwir.at[j, p, dx - 1], 7, m_dwi.at[j, p], dev(dx=dx))

    def dwi_x_all(j, p):
        return cp(dwir.at[j, p], dwir.at[j, p], 7, m_dwi.at[j, p], dev(dx=1))

    def dw_c(j):
        return cp(dwcs.at[j], dwcr.at[j], 8, m_dwc.at[j], dev(fc=1))

    def dx_s(p, d):
        return cp(dxss.at[p, d], dxsr.at[p, d], 9, m_dxs.at[p, d], dev(fs=1))

    def dx_y(p, d, dy):
        return cp(dxys.at[p, d, (y + dy) % 4], dxyr.at[p, d, dy - 1], 10, m_dxy.at[p, d], dev(dy=dy))

    def dx_y_all(p, d):
        return cp(dxyr.at[p, d], dxyr.at[p, d], 10, m_dxy.at[p, d], dev(dy=1))

    def dx_c(d):
        return cp(dxcs.at[d], dxcr.at[d], 11, m_dxc.at[d], dev(fc=1))

    def product(u):
        a, j, p = unit(u)
        lhs = tg[a, rows(half[p] * HALF, HALF)]
        pf[u % 4] = dot(lhs, wo[rows(j * CH, CH)], 1, 1) if a else dot(lhs, wi[j], 1, 0)

        def piece(owner, part):
            return pf[u % 4, rows(owner % 4 * OWN + part * TB, TB)].astype(BF16)

        s1s[u, 0, 0] = piece(k + 2, 0)
        s1s[u, 0, 1] = piece(k + 1, 1)
        s1(u, 0).start()
        s1s[u, 1, 0] = piece(k + 2, 1)
        s1s[u, 1, 1] = piece(k + 3, 0)
        s1(u, 1).start()

    def middle(u):
        for r in range(2):
            s1(u, r).wait_recv()
            own = pf[u % 4, rows((k + (1, 3)[r]) % 4 * OWN + r * TB, TB)]
            s2s[u, r] = (own + s1r[u, r, 0].astype(F32)).astype(BF16)
            s2(u, r).start()

    def finish(u):
        a, j, p = unit(u)
        for r in range(2):
            s2(u, r).wait_recv()
            value = pf[u % 4, rows(k * OWN + r * TB, TB)] + s2r[u, r].astype(F32) + s1r[u, 1 - r, 1].astype(F32)
            if a:
                value = value * slope[j, p, r]
            else:
                value, slope[j, p, r] = gelu_parts(value)
            hg[a, j, rows(half[p] * HALF + k * OWN + r * TB, TB)] = value.astype(BF16)
        for r in range(2):
            h1(u, r).start()

    def forward(u):
        for r in range(2):
            h1(u, r).wait_recv()
            h2(u, r).start()

    def arrived(u):
        for r in range(2):
            h2(u, r).wait_recv()

    def weight_out_part():
        for j in range(NJ):
            value = scale * dot(hg[0, j], tg[1], 0, 0)
            dwof[rows(j * CH, CH)] = value
            dwos[rows(j * CH, CH)] = value.astype(BF16)
        for d in (2, 1, 3):
            dwo_x(d).start()

    def weight_out_finish():
        dwo_x_all().wait_recv()
        value = dwof[rows(x * WB, WB)]
        for d in range(3):
            value = value + dwor[d].astype(F32)
        o_wout[...] = value.astype(BF16)

    def weight_in_part(j):
        value = scale * dot(tg[0], hg[1, j], 0, 0)
        dwif[j] = value
        dwis[j] = value.astype(BF16)
        for p in (1, 0):
            for d in (2, 1, 3):
                dwi_x(j, p, d).start()

    def weight_in_sum(j, p):
        dwi_x_all(j, p).wait_recv()
        value = dwif[j, rows((half[p] * 4 + x) * WB, WB)]
        for d in range(3):
            value = value + dwir[j, p, d].astype(F32)
        if p:
            dwcs[j] = value.astype(BF16)
            dw_c(j).start()
        else:
            o_win[:, pl.ds(pl.multiple_of(c * HID + j * CH, CH), CH)] = value.astype(BF16)

    def weight_in_finish(j):
        dw_c(j).wait_recv()
        o_win[:, pl.ds(pl.multiple_of(oc * HID + j * CH, CH), CH)] = dwcr[j]

    def cols(d):
        return pl.ds(d * DC, DC)

    def tokens_part(p, j, d):
        part = dot(hg[1, j, rows(half[p] * HALF, HALF)], wi[j, cols(d)], 1, 1)
        if j == 0:
            dxf[p, d] = part
        else:
            dxf[p, d] += part
        if j == NJ - 1:
            for yy in range(4):
                dxss[p, d, yy] = dxf[p, d, rows((yy * 2 + oco) * TB, TB)].astype(BF16)
            dx_s(p, d).start()

    def tokens_middle(p, d):
        dx_s(p, d).wait_recv()
        for yy in range(4):
            part = dxf[p, d, rows((yy * 2 + co) * TB, TB)] + dxsr[p, d, yy].astype(F32)
            dxyf[p, d, yy] = part
            dxys[p, d, yy] = part.astype(BF16)
        for dy in (2, 1, 3):
            dx_y(p, d, dy).start()

    def tokens_sum(p, d):
        dx_y_all(p, d).wait_recv()
        value = dxyf[p, d, y]
        for i in range(3):
            value = value + dxyr[p, d, i].astype(F32)
        if p:
            dxcs[d] = value.astype(BF16)
            dx_c(d).start()
        else:
            dx_c(d).wait_recv()
            o_tok[:, cols(d)] = (value + dxcr[d].astype(F32)).astype(BF16)

    local = [pltpu.make_async_copy((tok, cot)[a], tslot(a, c, y, co), m_loc.at[a]) for a in range(2)]
    local += [pltpu.make_async_copy(wcols(c, j), wslot(j, c, x), m_loc.at[2 + j]) for j in range(NJ)]
    local += [pltpu.make_async_copy(wout, wo.at[rows(x * WB, WB)], m_loc.at[5])]
    for copy in local:
        copy.start()
    barrier = pltpu.get_barrier_semaphore()
    partners = [dev(fs=1), dev(fc=1), dev(dk=1), dev(dk=3)]
    for d in (1, 2, 3):
        partners += [dev(dy=d), dev(dx=d)]
    for to in partners:
        pl.semaphore_signal(barrier, inc=1, device_id=to, device_id_type=MESH)
    pl.semaphore_wait(barrier, len(partners))

    ag_c(0).start()
    for d in (2, 1, 3):
        ag_y(0, 0, d).start()
        wi_x(0, 0, d).start()
    wi_c(0).start()
    ag_s(0, 0, 0).start()
    wi_c(1).start()
    wi_c(2).start()
    ag_c(1).start()
    ag_c(0).wait_recv()
    for d in (2, 1, 3):
        ag_y(0, 1, d).start()
    ag_s(0, 1, 0).start()
    wi_c(0).wait_recv()
    for d in (2, 1, 3):
        wi_x(0, 1, d).start()
    for d in (2, 1, 3):
        wi_x(1, 0, d).start()
    for d in (1, 3, 2):
        ag_y(0, 0, d).wait_recv()
        ag_s(0, 0, d).start()
    wi_c(1).wait_recv()
    for d in (2, 1, 3):
        wi_x(1, 1, d).start()
    for copy in local:
        copy.wait()
    ag_s_all(0, 0).wait_recv()
    wi_x_all(0).wait_recv()
    product(0)
    for d in (1, 3, 2):
        ag_y(0, 1, d).wait_recv()
        ag_s(0, 1, d).start()
    for d in (2, 1, 3):
        ag_y(1, 0, d).start()
    ag_s(1, 0, 0).start()
    wi_c(2).wait_recv()
    for p in (0, 1):
        for d in (2, 1, 3):
            wi_x(2, p, d).start()
    ag_c(1).wait_recv()
    for d in (2, 1, 3):
        ag_y(1, 1, d).start()
    ag_s(1, 1, 0).start()
    ag_s_all(0, 1).wait_recv()

    for t in range(1, 2 * NU + 4):
        if t == 2:
            wi_x_all(1).wait_recv()
            for d in (2, 1, 3):
                wo_x(d).start()
        if t == 4:
            wi_x_all(2).wait_recv()
        if t == NU:
            wo_x_all().wait_recv()
            for p in (0, 1):
                ag_s_all(1, p).wait_recv()
        if t < 2 * NU:
            product(t)
        if 0 <= t - 1 < 2 * NU:
            middle(t - 1)
        if 0 <= t - 2 < 2 * NU:
            finish(t - 2)
        if 0 <= t - 3 < 2 * NU:
            forward(t - 3)
        if t == 4:
            for p in (0, 1):
                for d in (1, 3, 2):
                    ag_y(1, p, d).wait_recv()
                    ag_s(1, p, d).start()
        if t == NU + 3:
            for u in range(NU):
                arrived(u)
            weight_out_part()
        u = t - 4
        if u >= NU:
            a, j, p = unit(u)
            arrived(u)
            if p:
                for d in range(ND):
                    tokens_part(1, j, d)
            elif j < NJ - 1:
                weight_in_part(j)
                for d in range(ND):
                    tokens_part(0, j, d)
                for d in range(ND):
                    (tokens_middle, tokens_sum)[j](1, d)
    for d in range(ND):
        tokens_part(0, NJ - 1, d)
    weight_in_part(NJ - 1)
    for d in range(ND):
        tokens_middle(0, d)
    weight_out_finish()
    for j in range(NJ):
        weight_in_sum(j, 1)
        if j < NJ - 1:
            weight_in_sum(j, 0)
    for d in range(ND):
        tokens_sum(0, d)
    weight_in_sum(NJ - 1, 0)
    for j in range(NJ):
        weight_in_finish(j)

    whole = (
        tg.at[:, pl.ds(0, 15 * TB)], wi.at[:, pl.ds(0, 7 * WB)], wo.at[pl.ds(0, 3 * WB)], s1s, s2s,
        hg.at[:, :, pl.ds(0, 6 * OWN)], dwor, dwir, dwcs, dxss, dxyr, dxcs,
    )
    for family, ref in enumerate(whole):
        cp(ref, ref, family, m_agc.at[0], dev(fs=1)).wait_send()


def shards(tokens, cotangent, weight_in, weight_out):
    scale = float(tokens.shape[0] * lax.axis_size("out") * lax.axis_size("dep")) ** (-0.5)
    vmem, dma = pltpu.VMEM, pltpu.SemaphoreType.DMA
    hbm = pl.BlockSpec(memory_space=pl.ANY)
    own = pl.BlockSpec(memory_space=pltpu.VMEM)
    return pl.pallas_call(
        functools.partial(kernel, scale),
        out_shape=tuple(jax.ShapeDtypeStruct(a.shape, BF16) for a in (tokens, weight_in, weight_out)),
        in_specs=[hbm] * 4,
        out_specs=(own,) * 3,
        scratch_shapes=[
            vmem((2, TOK, WID), BF16),
            vmem((NJ, WID, CH), BF16),
            vmem((HID, WID), BF16),
            vmem((4, HALF, CH), F32),
            vmem((2 * NU, 2, 2, TB, CH), BF16),
            vmem((2 * NU, 2, 2, TB, CH), BF16),
            vmem((2 * NU, 2, TB, CH), BF16),
            vmem((2 * NU, 2, TB, CH), BF16),
            vmem((2, NJ, TOK, CH), BF16),
            vmem((NJ, 2, 2, TB, CH), F32),
            vmem((HID, WID), F32),
            vmem((HID, WID), BF16),
            vmem((3, WB, WID), BF16),
            vmem((NJ, WID, CH), F32),
            vmem((NJ, WID, CH), BF16),
            vmem((NJ, 2, 3, WB, CH), BF16),
            vmem((NJ, WB, CH), BF16),
            vmem((NJ, WB, CH), BF16),
            vmem((2, ND, HALF, DC), F32),
            vmem((2, ND, 4, TB, DC), BF16),
            vmem((2, ND, 4, TB, DC), BF16),
            vmem((2, ND, 4, TB, DC), F32),
            vmem((2, ND, 4, TB, DC), BF16),
            vmem((2, ND, 3, TB, DC), BF16),
            vmem((ND, TB, DC), BF16),
            vmem((ND, TB, DC), BF16),
            dma((6,)),
            dma((12,)),
            dma((2,)),
            dma((2, 2, 3)),
            dma((2, 2)),
            dma((NJ,)),
            dma((NJ,)),
            dma,
            dma((2 * NU, 2)),
            dma((2 * NU, 2)),
            dma((2 * NU, 2)),
            dma((2 * NU, 2)),
            dma,
            dma((NJ, 2)),
            dma((NJ,)),
            dma((2, ND)),
            dma((2, ND)),
            dma((ND,)),
        ],
        compiler_params=pltpu.CompilerParams(
            collective_id=0, has_side_effects=True, vmem_limit_bytes=61 * 2**20
        ),
        cost_estimate=pl.CostEstimate(flops=11 * 10**9, bytes_accessed=3 * 10**6, transcendentals=0),
    )(tokens, cotangent, weight_in, weight_out)


def solution(mesh):
    in_specs = (
        P(("dep", "out"), "inp"),
        P(("dep", "out"), "inp"),
        P(("inp", "dep"), "out"),
        P(("out", "dep"), "inp"),
    )
    out_specs = (P(("dep", "out"), "inp"), P(("inp", "dep"), "out"), P(("out", "dep"), "inp"))
    return jax.shard_map(shards, mesh=mesh, in_specs=in_specs, out_specs=out_specs, check_vma=False)
```

time: 477 us -> 148 us (0.31)
  waiting for transfers between devices: 423 us -> 0 us
  Pallas kernels: 0 us -> 142 us
  matrix products: 25.8 us -> 0 us
  between operations: 14.2 us -> 0.64 us
    all_gather x4 -> x0, waiting for transfers between devices: 172 us -> none  [the longest x1 59.8 us: shards(): lax.all_gather(weight_out, 'dep', axis=0, tiled=True)]
    pallas_call x0 -> x1, Pallas kernels: none -> 142 us  [shards(): pl.pallas_call(functools.partial(kernel, scale), out_shape=tuple((jax.Sha...]
    psum x1 -> x0, waiting for transfers between devices: 109 us -> none  [shards(): lax.psum(preact_part.astype(jnp.bfloat16), 'inp').astype(jnp.float32)]
    reduce_scatter x2 -> x0, waiting for transfers between devices: 78.4 us -> none  [the longest x1 62.6 us: shards(): lax.psum_scatter(out_term.astype(jnp.bfloat16), 'dep', scatter_dimension=...]
    unnamed x9 -> x0, waiting for transfers between devices: 63 us -> none
    dot_general x5 -> x0, matrix products: 25.8 us -> none  [the longest x1 5.74 us: shards(): lax.dot_general(grads, lax.all_gather(weight_out, 'dep', axis=0, tiled=Tr...]
  transfers between devices with their start and end apart: 8 -> 0, of which waited for: 8 -> 0; matrix products, arithmetic and copies ran while one was open for 4% -> 0% of each run, Pallas kernels for 0% -> 0%
where the time goes in v2:
time: 148 us; the launch traced here: 147 us
  Pallas kernels  142 us (96%)
  local copies, waits for them, and re-layouts  4.38 us (3%)
    pallas_call x1, Pallas kernels, shards(): pl.pallas_call(functools.partial(kernel, scale), out_shape=tuple((jax.Sha...  142 us
    unnamed x5, local copies, waits for them, and re-layouts  4.38 us

profile of v2, /device:TPU:2, one launch (start us, length us, event | category | flops | bytes accessed | tf_op | source)
XLA Modules:
  0.0 147.4 jit_solution(1034075862133462189)
XLA Ops:
  0.6 142.4 %shard_map.67 = (bf16[48,1536]{1,0:T(8,128)(2,1)}, bf16[192,1536]{1,0:T(8,128)(2,1)}, bf16[192,1536]{1,0:T(8,128)(2,1)}) custom-call(bf16[48,1536]{1,0:T(8,128)(2,1)} %tok.1, bf16[48,1536]{1,0:T(8,128)(2,1)} %cot.1, bf16[192,1536]{1,0:T(8,128)(2,1)} %win.1, bf16[192,1536]{1,0:T(8,128)(2,1)} %wout.1), custom_call_target="tpu_custom_call" | custom-call | flops 11000000512 | bytes 3000000 | tf_op jit(solution)/shard_map/pallas_call | solution.py:392
  143.1 1.6 %copy.10 = bf16[48,1536]{1,0:T(8,128)(2,1)} copy(bf16[48,1536]{1,0:T(8,128)(2,1)} %get-tuple-element.6) | data formatting | bytes 294912
  144.6 0.0 copy-start
  144.6 2.0 %copy.11 = bf16[192,1536]{1,0:T(8,128)(2,1)} copy(bf16[192,1536]{1,0:T(8,128)(2,1)} %get-tuple-element.7) | data formatting | bytes 1179648
  146.6 0.0 copy-done
  146.6 0.8 copy.12
Async XLA Ops:
  144.6 2.0 %copy-start = (bf16[192,1536]{1,0:T(8,128)(2,1)S(1)}, bf16[192,1536]{1,0:T(8,128)(2,1)}, u32[]{:S(2)}) copy-start(bf16[192,1536]{1,0:T(8,128)(2,1)} %get-tuple-element.8) | copy-start | bytes 1769476

commit v3 on v2

--- a/solution.py
+++ b/solution.py
@@ -12,6 +12,7 @@
 NJ, CH = 3, 256
 NU = 2 * NJ
 ND, DC = 2, 768
+STEP = (1, 3)
 TB, WB = 48, 192
 TOK, WID, HID = 768, 1536, 768
 HALF, OWN = 384, 96
@@ -29,9 +30,10 @@
 
 def kernel(
     scale, tok, cot, win, wout, o_tok, o_win, o_wout,
-    tg, wi, wo, pf, s1s, s1r, s2s, s2r, hg, slope, dwof, dwos, dwor, dwif, dwis, dwir, dwcs, dwcr,
-    dxf, dxss, dxsr, dxyf, dxys, dxyr, dxcs, dxcr,
-    m_loc, sent, m_agc, m_agy, m_ags, m_wic, m_wix, m_wox, m_s1, m_s2, m_h1, m_h2, m_dwo, m_dwi, m_dwc, m_dxs, m_dxy, m_dxc,
+    tg, wi, wo, pf, s1s, s1r, s2s, s2r, hg, slope, dwof, o1s, o1r, o2s, o2r,
+    dwif, i1s, i1r, i2s, i2r, dwis, dwir, dwcs, dwcr, dxf, dxss, dxsr, dxyf, dxys, dxyr, dxcs, dxcr,
+    r_tok, r_win, r_wout, m_loc, m_res, sent, m_agc, m_agy, m_ags, m_wic, m_wix, m_wif, m_wox, m_wof, m_s1, m_s2, m_h1, m_h2,
+    m_o1, m_o2, m_i1, m_i2, m_dwi, m_dwc, m_dxs, m_dxy, m_dxc,
 ):
     k, out, dep = lax.axis_index("inp"), lax.axis_index("out"), lax.axis_index("dep")
     y, co, c, x = out // 2, out % 2, dep // 4, dep % 4
@@ -84,14 +86,27 @@
         return cp(slot if p else wcols(c, j), slot, 1, m_wix.at[j], dev(dx=dx))
 
     def wi_x_all(j):
-        ref = wi.at[j, pl.ds(0, 6 * WB)]
+        ref = wi.at[j, pl.ds(0, (4 if j else 6) * WB)]
         return cp(ref, ref, 1, m_wix.at[j], dev(dx=1))
 
-    def wo_x(dx):
-        return cp(wout, wo.at[rows(x * WB, WB)], 2, m_wox, dev(dx=dx))
-
-    def wo_x_all():
-        ref = wo.at[pl.ds(0, 3 * WB)]
+    def wi_n(j, p, r):
+        slot = wslot(j, half[p], x)
+        sem = m_wif.at[j, p] if p == r else m_wix.at[j]
+        return cp(slot if p else wcols(c, j), slot, 1, sem, dev(dx=STEP[r]))
+
+    def wi_f(j, p):
+        slot = wslot(j, half[p], (x + STEP[1 - p]) % 4)
+        return cp(slot, slot, 1, m_wix.at[j], dev(dx=STEP[p]))
+
+    def wo_n(r):
+        return cp(wout, wo.at[rows(x * WB, WB)], 2, m_wof.at[r], dev(dx=STEP[r]))
+
+    def wo_f(r):
+        slot = wo.at[rows((x + STEP[1 - r]) % 4 * WB + r * OWN, OWN)]
+        return cp(slot, slot, 2, m_wox, dev(dx=STEP[r]))
+
+    def wo_f_all():
+        ref = wo.at[pl.ds(0, WB)]
         return cp(ref, ref, 2, m_wox, dev(dx=1))
 
     def unit(u):
@@ -99,10 +114,10 @@
         return (0, i // 2, i % 2) if u < 6 else (1, i % 3, 1 - i // 3)
 
     def s1(u, r):
-        return cp(s1s.at[u, r], s1r.at[u, r], 3, m_s1.at[u, r], dev(dk=(1, 3)[r]))
+        return cp(s1s.at[u, r], s1r.at[u, r], 3, m_s1.at[u, r], dev(dk=STEP[r]))
 
     def s2(u, r):
-        return cp(s2s.at[u, r], s2r.at[u, r], 4, m_s2.at[u, r], dev(dk=(1, 3)[r]))
+        return cp(s2s.at[u, r], s2r.at[u, r], 4, m_s2.at[u, r], dev(dk=STEP[r]))
 
     def hrows(u, owner, part, n):
         a, j, p = unit(u)
@@ -110,24 +125,29 @@
 
     def h1(u, r):
         slot = hrows(u, k, 0, OWN)
-        return cp(slot, slot, 5, m_h1.at[u, r], dev(dk=(1, 3)[r]))
+        return cp(slot, slot, 5, m_h1.at[u, r], dev(dk=STEP[r]))
 
     def h2(u, r):
-        slot = hrows(u, k + (3, 1)[r], r, TB)
-        return cp(slot, slot, 5, m_h2.at[u, r], dev(dk=(1, 3)[r]))
-
-    def dwo_x(dx):
-        return cp(dwos.at[rows((x + dx) % 4 * WB, WB)], dwor.at[dx - 1], 6, m_dwo, dev(dx=dx))
-
-    def dwo_x_all():
-        return cp(dwor, dwor, 6, m_dwo, dev(dx=1))
-
-    def dwi_x(j, p, dx):
-        src = dwis.at[j, rows((half[p] * 4 + (x + dx) % 4) * WB, WB)]
-        return cp(src, dwir.at[j, p, dx - 1], 7, m_dwi.at[j, p], dev(dx=dx))
-
-    def dwi_x_all(j, p):
-        return cp(dwir.at[j, p], dwir.at[j, p], 7, m_dwi.at[j, p], dev(dx=1))
+        slot = hrows(u, k + STEP[1 - r], r, TB)
+        return cp(slot, slot, 5, m_h2.at[u, r], dev(dk=STEP[r]))
+
+    def o1(r):
+        return cp(o1s.at[r], o1r.at[r], 6, m_o1.at[r], dev(dx=STEP[r]))
+
+    def o2(r):
+        return cp(o2s.at[r], o2r.at[r], 7, m_o2.at[r], dev(dx=STEP[r]))
+
+    def i1(j, r):
+        return cp(i1s.at[j, r], i1r.at[j, r], 12, m_i1.at[j, r], dev(dx=STEP[r]))
+
+    def i2(j, r):
+        return cp(i2s.at[j, r], i2r.at[j, r], 13, m_i2.at[j, r], dev(dx=STEP[r]))
+
+    def dwi_x(p, dx):
+        return cp(dwis.at[p, dx - 1], dwir.at[p, dx - 1], 14, m_dwi.at[p], dev(dx=dx))
+
+    def dwi_x_all(p):
+        return cp(dwir.at[p], dwir.at[p], 14, m_dwi.at[p], dev(dx=1))
 
     def dw_c(j):
         return cp(dwcs.at[j], dwcr.at[j], 8, m_dwc.at[j], dev(fc=1))
@@ -162,7 +182,7 @@
     def middle(u):
         for r in range(2):
             s1(u, r).wait_recv()
-            own = pf[u % 4, rows((k + (1, 3)[r]) % 4 * OWN + r * TB, TB)]
+            own = pf[u % 4, rows((k + STEP[r]) % 4 * OWN + r * TB, TB)]
             s2s[u, r] = (own + s1r[u, r, 0].astype(F32)).astype(BF16)
             s2(u, r).start()
 
@@ -190,41 +210,77 @@
 
     def weight_out_part():
         for j in range(NJ):
-            value = scale * dot(hg[0, j], tg[1], 0, 0)
-            dwof[rows(j * CH, CH)] = value
-            dwos[rows(j * CH, CH)] = value.astype(BF16)
-        for d in (2, 1, 3):
-            dwo_x(d).start()
+            dwof[rows(j * CH, CH)] = scale * dot(hg[0, j], tg[1], 0, 0)
+
+        def piece(owner, part):
+            return dwof[rows(owner % 4 * WB + part * OWN, OWN)].astype(BF16)
+
+        for r in range(2):
+            o1s[r, 0] = piece(x + 2, r)
+            o1s[r, 1] = piece(x + STEP[r], 1 - r)
+            o1(r).start()
+
+    def weight_out_middle():
+        for r in range(2):
+            o1(r).wait_recv()
+            own = dwof[rows((x + STEP[r]) % 4 * WB + r * OWN, OWN)]
+            o2s[r] = (own + o1r[r, 0].astype(F32)).astype(BF16)
+            o2(r).start()
 
     def weight_out_finish():
-        dwo_x_all().wait_recv()
-        value = dwof[rows(x * WB, WB)]
-        for d in range(3):
-            value = value + dwor[d].astype(F32)
-        o_wout[...] = value.astype(BF16)
+        for r in range(2):
+            o2(r).wait_recv()
+            value = dwof[rows(x * WB + r * OWN, OWN)] + o2r[r].astype(F32) + o1r[1 - r, 1].astype(F32)
+            r_wout[pl.ds(r * OWN, OWN)] = value.astype(BF16)
+        result_out.start()
+
+    def weight_in_half(j, p):
+        value = scale * dot(tg[0, rows(half[p] * HALF, HALF)], hg[1, j, rows(half[p] * HALF, HALF)], 0, 0)
+        if p:
+            dwif[j] = value
+        else:
+            dwif[j] += value
+
+    def weight_in_piece(j, p, owner):
+        return dwif[j, rows((half[p] * 4 + owner % 4) * WB, WB)]
 
     def weight_in_part(j):
-        value = scale * dot(tg[0], hg[1, j], 0, 0)
-        dwif[j] = value
-        dwis[j] = value.astype(BF16)
-        for p in (1, 0):
-            for d in (2, 1, 3):
-                dwi_x(j, p, d).start()
+        weight_in_half(j, 0)
+        if j == NJ - 1:
+            for p in (1, 0):
+                for d in (2, 1, 3):
+                    dwis[p, d - 1] = weight_in_piece(j, p, x + d).astype(BF16)
+                    dwi_x(p, d).start()
+        else:
+            for r in range(2):
+                i1s[j, r, 0] = weight_in_piece(j, 1 - r, x + 2).astype(BF16)
+                i1s[j, r, 1] = weight_in_piece(j, r, x + STEP[r]).astype(BF16)
+                i1(j, r).start()
+
+    def weight_in_middle(j):
+        for r in range(2):
+            i1(j, r).wait_recv()
+            i2s[j, r] = (weight_in_piece(j, 1 - r, x + STEP[r]) + i1r[j, r, 0].astype(F32)).astype(BF16)
+            i2(j, r).start()
 
     def weight_in_sum(j, p):
-        dwi_x_all(j, p).wait_recv()
-        value = dwif[j, rows((half[p] * 4 + x) * WB, WB)]
-        for d in range(3):
-            value = value + dwir[j, p, d].astype(F32)
+        value = weight_in_piece(j, p, x)
+        if j == NJ - 1:
+            dwi_x_all(p).wait_recv()
+            for d in range(3):
+                value = value + dwir[p, d].astype(F32)
+        else:
+            i2(j, 1 - p).wait_recv()
+            value = value + i2r[j, 1 - p].astype(F32) + i1r[j, p, 1].astype(F32)
         if p:
             dwcs[j] = value.astype(BF16)
             dw_c(j).start()
         else:
-            o_win[:, pl.ds(pl.multiple_of(c * HID + j * CH, CH), CH)] = value.astype(BF16)
+            r_win[:, pl.ds(pl.multiple_of(c * HID + j * CH, CH), CH)] = value.astype(BF16)
 
     def weight_in_finish(j):
         dw_c(j).wait_recv()
-        o_win[:, pl.ds(pl.multiple_of(oc * HID + j * CH, CH), CH)] = dwcr[j]
+        r_win[:, pl.ds(pl.multiple_of(oc * HID + j * CH, CH), CH)] = dwcr[j]
 
     def cols(d):
         return pl.ds(d * DC, DC)
@@ -259,11 +315,13 @@
             dx_c(d).start()
         else:
             dx_c(d).wait_recv()
-            o_tok[:, cols(d)] = (value + dxcr[d].astype(F32)).astype(BF16)
+            r_tok[:, cols(d)] = (value + dxcr[d].astype(F32)).astype(BF16)
 
     local = [pltpu.make_async_copy((tok, cot)[a], tslot(a, c, y, co), m_loc.at[a]) for a in range(2)]
     local += [pltpu.make_async_copy(wcols(c, j), wslot(j, c, x), m_loc.at[2 + j]) for j in range(NJ)]
     local += [pltpu.make_async_copy(wout, wo.at[rows(x * WB, WB)], m_loc.at[5])]
+    results = ((r_tok, o_tok), (r_win, o_win), (r_wout, o_wout))
+    result_tok, result_in, result_out = [pltpu.make_async_copy(*pair, m_res.at[i]) for i, pair in enumerate(results)]
     for copy in local:
         copy.start()
     barrier = pltpu.get_barrier_semaphore()
@@ -274,67 +332,78 @@
         pl.semaphore_signal(barrier, inc=1, device_id=to, device_id_type=MESH)
     pl.semaphore_wait(barrier, len(partners))
 
+    wi_c(0).start()
+    for d in (2, 1, 3):
+        wi_x(0, 0, d).start()
+        ag_y(0, 0, d).start()
     ag_c(0).start()
-    for d in (2, 1, 3):
-        ag_y(0, 0, d).start()
-        wi_x(0, 0, d).start()
-    wi_c(0).start()
     ag_s(0, 0, 0).start()
     wi_c(1).start()
     wi_c(2).start()
     ag_c(1).start()
+    wi_c(0).wait_recv()
+    for d in (2, 1, 3):
+        wi_x(0, 1, d).start()
+    for r in range(2):
+        wi_n(1, 0, r).start()
     ag_c(0).wait_recv()
     for d in (2, 1, 3):
         ag_y(0, 1, d).start()
     ag_s(0, 1, 0).start()
-    wi_c(0).wait_recv()
-    for d in (2, 1, 3):
-        wi_x(0, 1, d).start()
-    for d in (2, 1, 3):
-        wi_x(1, 0, d).start()
     for d in (1, 3, 2):
         ag_y(0, 0, d).wait_recv()
         ag_s(0, 0, d).start()
     wi_c(1).wait_recv()
-    for d in (2, 1, 3):
-        wi_x(1, 1, d).start()
+    for r in range(2):
+        wi_n(1, 1, r).start()
     for copy in local:
         copy.wait()
     ag_s_all(0, 0).wait_recv()
     wi_x_all(0).wait_recv()
     product(0)
+    for p in range(2):
+        m = cp(wslot(1, 0, 0), wslot(1, 0, 0), 1, m_wif.at[1, p], dev(dx=1))
+        m.wait_recv()
+        wi_f(1, p).start()
+    wi_c(2).wait_recv()
+    for p in range(2):
+        for r in range(2):
+            wi_n(2, p, r).start()
     for d in (1, 3, 2):
         ag_y(0, 1, d).wait_recv()
         ag_s(0, 1, d).start()
     for d in (2, 1, 3):
         ag_y(1, 0, d).start()
     ag_s(1, 0, 0).start()
-    wi_c(2).wait_recv()
-    for p in (0, 1):
-        for d in (2, 1, 3):
-            wi_x(2, p, d).start()
     ag_c(1).wait_recv()
     for d in (2, 1, 3):
         ag_y(1, 1, d).start()
     ag_s(1, 1, 0).start()
     ag_s_all(0, 1).wait_recv()
-
-    for t in range(1, 2 * NU + 4):
+    product(1)
+    middle(0)
+    for r in range(2):
+        wo_n(r).start()
+
+    for t in range(2, 2 * NU + 4):
         if t == 2:
             wi_x_all(1).wait_recv()
-            for d in (2, 1, 3):
-                wo_x(d).start()
+        if t == 3:
+            for p in range(2):
+                m = cp(wslot(2, 0, 0), wslot(2, 0, 0), 1, m_wif.at[2, p], dev(dx=1))
+                m.wait_recv()
+                wi_f(2, p).start()
         if t == 4:
             wi_x_all(2).wait_recv()
         if t == NU:
-            wo_x_all().wait_recv()
+            wo_f_all().wait_recv()
             for p in (0, 1):
                 ag_s_all(1, p).wait_recv()
         if t < 2 * NU:
             product(t)
-        if 0 <= t - 1 < 2 * NU:
+        if t - 1 < 2 * NU:
             middle(t - 1)
-        if 0 <= t - 2 < 2 * NU:
+        if t - 2 < 2 * NU:
             finish(t - 2)
         if 0 <= t - 3 < 2 * NU:
             forward(t - 3)
@@ -343,15 +412,22 @@
                 for d in (1, 3, 2):
                     ag_y(1, p, d).wait_recv()
                     ag_s(1, p, d).start()
+        if t == NU - 1:
+            for r in range(2):
+                wo_n(r).wait_recv()
+                wo_f(r).start()
         if t == NU + 3:
             for u in range(NU):
                 arrived(u)
             weight_out_part()
+        if t == NU + 5:
+            weight_out_middle()
         u = t - 4
         if u >= NU:
             a, j, p = unit(u)
             arrived(u)
             if p:
+                weight_in_half(j, 1)
                 for d in range(ND):
                     tokens_part(1, j, d)
             elif j < NJ - 1:
@@ -360,40 +436,56 @@
                     tokens_part(0, j, d)
                 for d in range(ND):
                     (tokens_middle, tokens_sum)[j](1, d)
+                if j == 1:
+                    weight_in_middle(0)
     for d in range(ND):
         tokens_part(0, NJ - 1, d)
     weight_in_part(NJ - 1)
+    weight_in_middle(1)
     for d in range(ND):
         tokens_middle(0, d)
     weight_out_finish()
-    for j in range(NJ):
+    for j in range(NJ - 1):
         weight_in_sum(j, 1)
-        if j < NJ - 1:
-            weight_in_sum(j, 0)
+        weight_in_sum(j, 0)
+    weight_in_sum(NJ - 1, 1)
     for d in range(ND):
         tokens_sum(0, d)
+    result_tok.start()
     weight_in_sum(NJ - 1, 0)
     for j in range(NJ):
         weight_in_finish(j)
+    result_in.start()
 
     whole = (
         tg.at[:, pl.ds(0, 15 * TB)], wi.at[:, pl.ds(0, 7 * WB)], wo.at[pl.ds(0, 3 * WB)], s1s, s2s,
-        hg.at[:, :, pl.ds(0, 6 * OWN)], dwor, dwir, dwcs, dxss, dxyr, dxcs,
+        hg.at[:, :, pl.ds(0, 6 * OWN)], o1s, o2s, dwcs, dxss, dxyr, dxcs, i1s, i2s, dwis,
     )
     for family, ref in enumerate(whole):
         cp(ref, ref, family, m_agc.at[0], dev(fs=1)).wait_send()
+    for copy in (result_tok, result_in, result_out):
+        copy.wait()
+
+
+def hand_over(*refs):
+    sems = refs[6]
+    copies = [pltpu.make_async_copy(refs[i], refs[3 + i], sems.at[i]) for i in range(3)]
+    for copy in copies:
+        copy.start()
+    for copy in copies:
+        copy.wait()
 
 
 def shards(tokens, cotangent, weight_in, weight_out):
     scale = float(tokens.shape[0] * lax.axis_size("out") * lax.axis_size("dep")) ** (-0.5)
     vmem, dma = pltpu.VMEM, pltpu.SemaphoreType.DMA
     hbm = pl.BlockSpec(memory_space=pl.ANY)
-    own = pl.BlockSpec(memory_space=pltpu.VMEM)
-    return pl.pallas_call(
+    shapes = tuple(jax.ShapeDtypeStruct(a.shape, BF16) for a in (tokens, weight_in, weight_out))
+    results = pl.pallas_call(
         functools.partial(kernel, scale),
-        out_shape=tuple(jax.ShapeDtypeStruct(a.shape, BF16) for a in (tokens, weight_in, weight_out)),
+        out_shape=shapes,
         in_specs=[hbm] * 4,
-        out_specs=(own,) * 3,
+        out_specs=(hbm,) * 3,
         scratch_shapes=[
             vmem((2, TOK, WID), BF16),
             vmem((NJ, WID, CH), BF16),
@@ -406,11 +498,17 @@
             vmem((2, NJ, TOK, CH), BF16),
             vmem((NJ, 2, 2, TB, CH), F32),
             vmem((HID, WID), F32),
-            vmem((HID, WID), BF16),
-            vmem((3, WB, WID), BF16),
+            vmem((2, 2, OWN, WID), BF16),
+            vmem((2, 2, OWN, WID), BF16),
+            vmem((2, OWN, WID), BF16),
+            vmem((2, OWN, WID), BF16),
             vmem((NJ, WID, CH), F32),
-            vmem((NJ, WID, CH), BF16),
-            vmem((NJ, 2, 3, WB, CH), BF16),
+            vmem((NJ - 1, 2, 2, WB, CH), BF16),
+            vmem((NJ - 1, 2, 2, WB, CH), BF16),
+            vmem((NJ - 1, 2, WB, CH), BF16),
+            vmem((NJ - 1, 2, WB, CH), BF16),
+            vmem((2, 3, WB, CH), BF16),
+            vmem((2, 3, WB, CH), BF16),
             vmem((NJ, WB, CH), BF16),
             vmem((NJ, WB, CH), BF16),
             vmem((2, ND, HALF, DC), F32),
@@ -421,20 +519,29 @@
             vmem((2, ND, 3, TB, DC), BF16),
             vmem((ND, TB, DC), BF16),
             vmem((ND, TB, DC), BF16),
+            vmem((TB, WID), BF16),
+            vmem((WB, WID), BF16),
+            vmem((WB, WID), BF16),
             dma((6,)),
-            dma((12,)),
+            dma((3,)),
+            dma((15,)),
             dma((2,)),
             dma((2, 2, 3)),
             dma((2, 2)),
             dma((NJ,)),
             dma((NJ,)),
+            dma((NJ, 2)),
             dma,
+            dma((2,)),
             dma((2 * NU, 2)),
             dma((2 * NU, 2)),
             dma((2 * NU, 2)),
             dma((2 * NU, 2)),
-            dma,
-            dma((NJ, 2)),
+            dma((2,)),
+            dma((2,)),
+            dma((NJ - 1, 2)),
+            dma((NJ - 1, 2)),
+            dma((2,)),
             dma((NJ,)),
             dma((2, ND)),
             dma((2, ND)),
@@ -445,6 +552,9 @@
         ),
         cost_estimate=pl.CostEstimate(flops=11 * 10**9, bytes_accessed=3 * 10**6, transcendentals=0),
     )(tokens, cotangent, weight_in, weight_out)
+    return pl.pallas_call(
+        hand_over, out_shape=shapes, in_specs=[hbm] * 3, out_specs=(hbm,) * 3, scratch_shapes=[dma((3,))]
+    )(*results)
 
 
 def solution(mesh):

time: 148 us -> 182 us (1.23)
  Pallas kernels: 142 us -> 181 us
  local copies, waits for them, and re-layouts: 4.38 us -> 0 us
    pallas_call x1 -> x2, Pallas kernels: 142 us -> 181 us  [the longest x1 140 us: shards(): pl.pallas_call(functools.partial(kernel, scale), out_shape=shapes, in_spe...]
    unnamed x5 -> x0, local copies, waits for them, and re-layouts: 4.38 us -> none
where the time goes in v3:
time: 182 us
  Pallas kernels  181 us (99%)
    pallas_call x1, Pallas kernels, shards(): pl.pallas_call(functools.partial(kernel, scale), out_shape=shapes, in_spe...  140 us
    pallas_call x1, Pallas kernels, shards(): pl.pallas_call(hand_over, out_shape=shapes, in_specs=[hbm] * 3, out_specs...  41.3 us

profile of v3, /device:TPU:2, one launch (start us, length us, event | category | flops | bytes accessed | tf_op | source)
XLA Modules:
  0.0 182.1 jit_solution(16969306256251784409)
XLA Ops:
  0.6 140.0 %shard_map.67 = (bf16[48,1536]{1,0:T(8,128)(2,1)}, bf16[192,1536]{1,0:T(8,128)(2,1)}, bf16[192,1536]{1,0:T(8,128)(2,1)}) custom-call(bf16[48,1536]{1,0:T(8,128)(2,1)} %tok.1, bf16[48,1536]{1,0:T(8,128)(2,1)} %cot.1, bf16[192,1536]{1,0:T(8,128)(2,1)} %win.1, bf16[192,1536]{1,0:T(8,128)(2,1)} %wout.1), custom_call_target="tpu_custom_call" | custom-call | flops 11000000512 | bytes 3000000 | tf_op jit(solution)/shard_map/pallas_call | solution.py:484
  140.6 41.3 %shard_map.68 = (bf16[48,1536]{1,0:T(8,128)(2,1)}, bf16[192,1536]{1,0:T(8,128)(2,1)}, bf16[192,1536]{1,0:T(8,128)(2,1)}) custom-call(bf16[48,1536]{1,0:T(8,128)(2,1)} %get-tuple-element.6.refs_0_, bf16[192,1536]{1,0:T(8,128)(2,1)} %get-tuple-element.7.refs_1_, bf16[192,1536]{1,0:T(8,128)(2,1)} %get-tuple-element.8.refs_2_), custom_call_target="tpu_custom_call" | custom-call | tf_op jit(solution)/shard_map/pallas_call | solution.py:555

commit v4 on v3

--- a/solution.py
+++ b/solution.py
@@ -11,7 +11,9 @@
 BF16, F32 = jnp.bfloat16, jnp.float32
 NJ, CH = 3, 256
 NU = 2 * NJ
+ORDER = ((0, 1), (0, 0), (1, 1), (1, 0), (2, 1), (2, 0))
 ND, DC = 2, 768
+OB, OH = 64, 32
 STEP = (1, 3)
 TB, WB = 48, 192
 TOK, WID, HID = 768, 1536, 768
@@ -30,7 +32,7 @@
 
 def kernel(
     scale, tok, cot, win, wout, o_tok, o_win, o_wout,
-    tg, wi, wo, pf, s1s, s1r, s2s, s2r, hg, slope, dwof, o1s, o1r, o2s, o2r,
+    tg, wl, wst, wi, wo, pf, s1s, s1r, s2s, s2r, hg, slope, dwof, o1s, o1r, o2s, o2r,
     dwif, i1s, i1r, i2s, i2r, dwis, dwir, dwcs, dwcr, dxf, dxss, dxsr, dxyf, dxys, dxyr, dxcs, dxcr,
     r_tok, r_win, r_wout, m_loc, m_res, sent, m_agc, m_agy, m_ags, m_wic, m_wix, m_wif, m_wox, m_wof, m_s1, m_s2, m_h1, m_h2,
     m_o1, m_o2, m_i1, m_i2, m_dwi, m_dwc, m_dxs, m_dxy, m_dxc,
@@ -75,15 +77,12 @@
     def wslot(j, cc, xx):
         return wi.at[j, rows((cc * 4 + xx) * WB, WB)]
 
-    def wcols(cc, j):
-        return win.at[:, pl.ds(pl.multiple_of(cc * HID + j * CH, CH), CH)]
-
     def wi_c(j):
-        return cp(wcols(oc, j), wslot(j, c, x), 1, m_wic.at[j], dev(fc=1))
+        return cp(wst.at[oc, j], wslot(j, c, x), 1, m_wic.at[j], dev(fc=1))
 
     def wi_x(j, p, dx):
         slot = wslot(j, half[p], x)
-        return cp(slot if p else wcols(c, j), slot, 1, m_wix.at[j], dev(dx=dx))
+        return cp(slot if p else wst.at[c, j], slot, 1, m_wix.at[j], dev(dx=dx))
 
     def wi_x_all(j):
         ref = wi.at[j, pl.ds(0, (4 if j else 6) * WB)]
@@ -92,26 +91,47 @@
     def wi_n(j, p, r):
         slot = wslot(j, half[p], x)
         sem = m_wif.at[j, p] if p == r else m_wix.at[j]
-        return cp(slot if p else wcols(c, j), slot, 1, sem, dev(dx=STEP[r]))
+        return cp(slot if p else wst.at[c, j], slot, 1, sem, dev(dx=STEP[r]))
 
     def wi_f(j, p):
         slot = wslot(j, half[p], (x + STEP[1 - p]) % 4)
         return cp(slot, slot, 1, m_wix.at[j], dev(dx=STEP[p]))
 
-    def wo_n(r):
-        return cp(wout, wo.at[rows(x * WB, WB)], 2, m_wof.at[r], dev(dx=STEP[r]))
-
-    def wo_f(r):
-        slot = wo.at[rows((x + STEP[1 - r]) % 4 * WB + r * OWN, OWN)]
-        return cp(slot, slot, 2, m_wox, dev(dx=STEP[r]))
-
-    def wo_f_all():
-        ref = wo.at[pl.ds(0, WB)]
-        return cp(ref, ref, 2, m_wox, dev(dx=1))
+    def wi_pass_on(j):
+        slot = wslot(j, 0, 0)
+        for p in range(2):
+            cp(slot, slot, 1, m_wif.at[j, p], dev(dx=1)).wait_recv()
+            wi_f(j, p).start()
+
+    def wo_part(j, xx, part):
+        return wo.at[j, rows(xx % 4 * OB + part * OH, OH)]
+
+    def wo_n(j, r, part):
+        sem = m_wof.at[j, r] if part == r else m_wox.at[j]
+        src = wout.at[pl.ds(j * OB + part * OH, OH)]
+        return cp(src, wo_part(j, x, part), 2, sem, dev(dx=STEP[r]))
+
+    def wo_f(j, r):
+        slot = wo_part(j, x + STEP[1 - r], r)
+        return cp(slot, slot, 2, m_wox.at[j], dev(dx=STEP[r]))
+
+    def wo_all(j):
+        ref = wo.at[j, pl.ds(0, 4 * OH)]
+        return cp(ref, ref, 2, m_wox.at[j], dev(dx=1))
+
+    def wo_send(j):
+        for i in range(2):
+            for r in range(2):
+                wo_n(j, r, (r + i) % 2).start()
+
+    def wo_pass_on(j):
+        for r in range(2):
+            wo_n(j, r, r).wait_recv()
+            wo_f(j, r).start()
 
     def unit(u):
-        i = u % 6
-        return (0, i // 2, i % 2) if u < 6 else (1, i % 3, 1 - i // 3)
+        a, i = divmod(u, NU)
+        return (a, *ORDER[i]) if a else (a, i // 2, i % 2)
 
     def s1(u, r):
         return cp(s1s.at[u, r], s1r.at[u, r], 3, m_s1.at[u, r], dev(dk=STEP[r]))
@@ -131,11 +151,11 @@
         slot = hrows(u, k + STEP[1 - r], r, TB)
         return cp(slot, slot, 5, m_h2.at[u, r], dev(dk=STEP[r]))
 
-    def o1(r):
-        return cp(o1s.at[r], o1r.at[r], 6, m_o1.at[r], dev(dx=STEP[r]))
-
-    def o2(r):
-        return cp(o2s.at[r], o2r.at[r], 7, m_o2.at[r], dev(dx=STEP[r]))
+    def o1(j, r):
+        return cp(o1s.at[j, r], o1r.at[j, r], 6, m_o1.at[j, r], dev(dx=STEP[r]))
+
+    def o2(j, r):
+        return cp(o2s.at[j, r], o2r.at[j, r], 7, m_o2.at[j, r], dev(dx=STEP[r]))
 
     def i1(j, r):
         return cp(i1s.at[j, r], i1r.at[j, r], 12, m_i1.at[j, r], dev(dx=STEP[r]))
@@ -167,7 +187,7 @@
     def product(u):
         a, j, p = unit(u)
         lhs = tg[a, rows(half[p] * HALF, HALF)]
-        pf[u % 4] = dot(lhs, wo[rows(j * CH, CH)], 1, 1) if a else dot(lhs, wi[j], 1, 0)
+        pf[u % 4] = dot(lhs, wo[j], 1, 1) if a else dot(lhs, wi[j], 1, 0)
 
         def piece(owner, part):
             return pf[u % 4, rows(owner % 4 * OWN + part * TB, TB)].astype(BF16)
@@ -208,31 +228,29 @@
         for r in range(2):
             h2(u, r).wait_recv()
 
-    def weight_out_part():
-        for j in range(NJ):
-            dwof[rows(j * CH, CH)] = scale * dot(hg[0, j], tg[1], 0, 0)
+    def weight_out_part(j):
+        dwof[j] = scale * dot(hg[0, j], tg[1], 0, 0)
 
         def piece(owner, part):
-            return dwof[rows(owner % 4 * WB + part * OWN, OWN)].astype(BF16)
-
-        for r in range(2):
-            o1s[r, 0] = piece(x + 2, r)
-            o1s[r, 1] = piece(x + STEP[r], 1 - r)
-            o1(r).start()
-
-    def weight_out_middle():
-        for r in range(2):
-            o1(r).wait_recv()
-            own = dwof[rows((x + STEP[r]) % 4 * WB + r * OWN, OWN)]
-            o2s[r] = (own + o1r[r, 0].astype(F32)).astype(BF16)
-            o2(r).start()
-
-    def weight_out_finish():
-        for r in range(2):
-            o2(r).wait_recv()
-            value = dwof[rows(x * WB + r * OWN, OWN)] + o2r[r].astype(F32) + o1r[1 - r, 1].astype(F32)
-            r_wout[pl.ds(r * OWN, OWN)] = value.astype(BF16)
-        result_out.start()
+            return dwof[j, rows(owner % 4 * OB + part * OH, OH)].astype(BF16)
+
+        for r in range(2):
+            o1s[j, r, 0] = piece(x + 2, r)
+            o1s[j, r, 1] = piece(x + STEP[r], 1 - r)
+            o1(j, r).start()
+
+    def weight_out_middle(j):
+        for r in range(2):
+            o1(j, r).wait_recv()
+            own = dwof[j, rows((x + STEP[r]) % 4 * OB + r * OH, OH)]
+            o2s[j, r] = (own + o1r[j, r, 0].astype(F32)).astype(BF16)
+            o2(j, r).start()
+
+    def weight_out_finish(j):
+        for r in range(2):
+            o2(j, r).wait_recv()
+            value = dwof[j, rows(x * OB + r * OH, OH)] + o2r[j, r].astype(F32) + o1r[j, 1 - r, 1].astype(F32)
+            r_wout[pl.ds(j * OB + r * OH, OH)] = value.astype(BF16)
 
     def weight_in_half(j, p):
         value = scale * dot(tg[0, rows(half[p] * HALF, HALF)], hg[1, j, rows(half[p] * HALF, HALF)], 0, 0)
@@ -262,6 +280,10 @@
             i1(j, r).wait_recv()
             i2s[j, r] = (weight_in_piece(j, 1 - r, x + STEP[r]) + i1r[j, r, 0].astype(F32)).astype(BF16)
             i2(j, r).start()
+
+    def weight_in_result(cc, j, value):
+        for xx in range(4):
+            r_win[cc, :, pl.ds(xx * WB + j * OB, OB)] = value[:, xx * OB : (xx + 1) * OB]
 
     def weight_in_sum(j, p):
         value = weight_in_piece(j, p, x)
@@ -276,11 +298,11 @@
             dwcs[j] = value.astype(BF16)
             dw_c(j).start()
         else:
-            r_win[:, pl.ds(pl.multiple_of(c * HID + j * CH, CH), CH)] = value.astype(BF16)
+            weight_in_result(c, j, value.astype(BF16))
 
     def weight_in_finish(j):
         dw_c(j).wait_recv()
-        r_win[:, pl.ds(pl.multiple_of(oc * HID + j * CH, CH), CH)] = dwcr[j]
+        weight_in_result(oc, j, dwcr[j])
 
     def cols(d):
         return pl.ds(d * DC, DC)
@@ -318,10 +340,12 @@
             r_tok[:, cols(d)] = (value + dxcr[d].astype(F32)).astype(BF16)
 
     local = [pltpu.make_async_copy((tok, cot)[a], tslot(a, c, y, co), m_loc.at[a]) for a in range(2)]
-    local += [pltpu.make_async_copy(wcols(c, j), wslot(j, c, x), m_loc.at[2 + j]) for j in range(NJ)]
-    local += [pltpu.make_async_copy(wout, wo.at[rows(x * WB, WB)], m_loc.at[5])]
-    results = ((r_tok, o_tok), (r_win, o_win), (r_wout, o_wout))
-    result_tok, result_in, result_out = [pltpu.make_async_copy(*pair, m_res.at[i]) for i, pair in enumerate(results)]
+    local += [pltpu.make_async_copy(wout.at[pl.ds(j * OB, OB)], wo.at[j, rows(x * OB, OB)], m_loc.at[2 + j]) for j in range(NJ)]
+    columns = pltpu.make_async_copy(win, wl, m_loc.at[5])
+    result_tok = pltpu.make_async_copy(r_tok, o_tok, m_res.at[0])
+    result_out = pltpu.make_async_copy(r_wout, o_wout, m_res.at[1])
+    result_in = [pltpu.make_async_copy(r_win.at[i], o_win.at[:, pl.ds(i * HID, HID)], m_res.at[2 + i]) for i in range(2)]
+    columns.start()
     for copy in local:
         copy.start()
     barrier = pltpu.get_barrier_semaphore()
@@ -330,6 +354,12 @@
         partners += [dev(dy=d), dev(dx=d)]
     for to in partners:
         pl.semaphore_signal(barrier, inc=1, device_id=to, device_id_type=MESH)
+    columns.wait()
+    for j in range(NJ):
+        for cc in range(2):
+            for xx in range(4):
+                wst[cc, j, :, pl.ds(xx * OB, OB)] = wl[:, pl.ds(cc * HID + xx * WB + j * OB, OB)]
+        wi[j, rows((c * 4 + x) * WB, WB)] = wst[c, j]
     pl.semaphore_wait(barrier, len(partners))
 
     wi_c(0).start()
@@ -356,22 +386,20 @@
     wi_c(1).wait_recv()
     for r in range(2):
         wi_n(1, 1, r).start()
+    for r in range(2):
+        wi_n(2, 0, r).start()
     for copy in local:
         copy.wait()
     ag_s_all(0, 0).wait_recv()
     wi_x_all(0).wait_recv()
     product(0)
-    for p in range(2):
-        m = cp(wslot(1, 0, 0), wslot(1, 0, 0), 1, m_wif.at[1, p], dev(dx=1))
-        m.wait_recv()
-        wi_f(1, p).start()
     wi_c(2).wait_recv()
-    for p in range(2):
-        for r in range(2):
-            wi_n(2, p, r).start()
+    for r in range(2):
+        wi_n(2, 1, r).start()
     for d in (1, 3, 2):
         ag_y(0, 1, d).wait_recv()
         ag_s(0, 1, d).start()
+    wi_pass_on(1)
     for d in (2, 1, 3):
         ag_y(1, 0, d).start()
     ag_s(1, 0, 0).start()
@@ -381,98 +409,104 @@
     ag_s(1, 1, 0).start()
     ag_s_all(0, 1).wait_recv()
     product(1)
-    middle(0)
-    for r in range(2):
-        wo_n(r).start()
-
-    for t in range(2, 2 * NU + 4):
-        if t == 2:
-            wi_x_all(1).wait_recv()
-        if t == 3:
-            for p in range(2):
-                m = cp(wslot(2, 0, 0), wslot(2, 0, 0), 1, m_wif.at[2, p], dev(dx=1))
-                m.wait_recv()
-                wi_f(2, p).start()
-        if t == 4:
-            wi_x_all(2).wait_recv()
-        if t == NU:
-            wo_f_all().wait_recv()
-            for p in (0, 1):
-                ag_s_all(1, p).wait_recv()
-        if t < 2 * NU:
-            product(t)
+
+    for t in range(1, 2 * NU + 4):
         if t - 1 < 2 * NU:
             middle(t - 1)
-        if t - 2 < 2 * NU:
+        if 0 <= t - 2 < 2 * NU:
             finish(t - 2)
         if 0 <= t - 3 < 2 * NU:
             forward(t - 3)
-        if t == 4:
+        if t == 1:
+            wi_x_all(1).wait_recv()
+        if t == 3:
+            wi_x_all(2).wait_recv()
+        if t == NU - 1:
+            for p in (0, 1):
+                ag_s_all(1, p).wait_recv()
+        if t >= NU - 1 and (t + 1 - NU) % 2 == 0 and t + 1 < 2 * NU:
+            wo_all((t + 1 - NU) // 2).wait_recv()
+        if t + 1 < 2 * NU:
+            product(t + 1)
+        if t == 1:
+            wo_send(0)
+        if t == 2:
+            wi_pass_on(2)
+            wo_send(1)
+        if t == 3:
             for p in (0, 1):
                 for d in (1, 3, 2):
                     ag_y(1, p, d).wait_recv()
                     ag_s(1, p, d).start()
-        if t == NU - 1:
-            for r in range(2):
-                wo_n(r).wait_recv()
-                wo_f(r).start()
-        if t == NU + 3:
-            for u in range(NU):
-                arrived(u)
-            weight_out_part()
-        if t == NU + 5:
-            weight_out_middle()
+            wo_pass_on(0)
+            wo_send(2)
+        if t in (4, 5):
+            wo_pass_on(t - 3)
+        for j in range(NJ):
+            if t == 2 * j + 5:
+                arrived(2 * j)
+                arrived(2 * j + 1)
+                weight_out_part(j)
+            if t == 2 * j + 6:
+                weight_out_middle(j)
+            if t == 2 * j + 8:
+                weight_out_finish(j)
+        if t == 2 * NU:
+            result_out.start()
         u = t - 4
+        if u == NU + 5:
+            for d in range(ND):
+                tokens_middle(1, d)
         if u >= NU:
             a, j, p = unit(u)
             arrived(u)
             if p:
                 weight_in_half(j, 1)
-                for d in range(ND):
-                    tokens_part(1, j, d)
-            elif j < NJ - 1:
+            for d in range(ND):
+                tokens_part(p, j, d)
+            if not p:
                 weight_in_part(j)
-                for d in range(ND):
-                    tokens_part(0, j, d)
-                for d in range(ND):
-                    (tokens_middle, tokens_sum)[j](1, d)
-                if j == 1:
-                    weight_in_middle(0)
-    for d in range(ND):
-        tokens_part(0, NJ - 1, d)
-    weight_in_part(NJ - 1)
-    weight_in_middle(1)
+            if u == NU + 2:
+                weight_in_middle(0)
     for d in range(ND):
         tokens_middle(0, d)
-    weight_out_finish()
-    for j in range(NJ - 1):
-        weight_in_sum(j, 1)
-        weight_in_sum(j, 0)
-    weight_in_sum(NJ - 1, 1)
+    weight_in_middle(1)
+    for p in (1, 0):
+        weight_in_sum(0, p)
+    for d in range(ND):
+        tokens_sum(1, d)
+    weight_in_sum(2, 1)
+    for p in (1, 0):
+        weight_in_sum(1, p)
     for d in range(ND):
         tokens_sum(0, d)
     result_tok.start()
-    weight_in_sum(NJ - 1, 0)
+    weight_in_sum(2, 0)
     for j in range(NJ):
         weight_in_finish(j)
-    result_in.start()
+    for copy in result_in:
+        copy.start()
 
     whole = (
-        tg.at[:, pl.ds(0, 15 * TB)], wi.at[:, pl.ds(0, 7 * WB)], wo.at[pl.ds(0, 3 * WB)], s1s, s2s,
+        tg.at[:, pl.ds(0, 15 * TB)], wi.at[:, pl.ds(0, 7 * WB)], wo.at[:, pl.ds(0, 3 * OB)], s1s, s2s,
         hg.at[:, :, pl.ds(0, 6 * OWN)], o1s, o2s, dwcs, dxss, dxyr, dxcs, i1s, i2s, dwis,
     )
     for family, ref in enumerate(whole):
         cp(ref, ref, family, m_agc.at[0], dev(fs=1)).wait_send()
-    for copy in (result_tok, result_in, result_out):
+    for copy in (result_tok, result_out, *result_in):
         copy.wait()
 
 
 def hand_over(*refs):
-    sems = refs[6]
-    copies = [pltpu.make_async_copy(refs[i], refs[3 + i], sems.at[i]) for i in range(3)]
-    for copy in copies:
+    sems = refs[9]
+    loads = [pltpu.make_async_copy(refs[i], refs[6 + i], sems.at[i]) for i in range(3)]
+    stores = [pltpu.make_async_copy(refs[6 + i], refs[3 + i], sems.at[3 + i]) for i in range(3)]
+    for copy in loads:
         copy.start()
-    for copy in copies:
+    for load, store in zip(loads, stores):
+        load.wait()
+        store.start()
+    for copy in stores:
         copy.wait()
 
 
@@ -488,8 +522,10 @@
         out_specs=(hbm,) * 3,
         scratch_shapes=[
             vmem((2, TOK, WID), BF16),
+            vmem((WB, 2 * HID), BF16),
+            vmem((2, NJ, WB, CH), BF16),
             vmem((NJ, WID, CH), BF16),
-            vmem((HID, WID), BF16),
+            vmem((NJ, CH, WID), BF16),
             vmem((4, HALF, CH), F32),
             vmem((2 * NU, 2, 2, TB, CH), BF16),
             vmem((2 * NU, 2, 2, TB, CH), BF16),
@@ -497,11 +533,11 @@
             vmem((2 * NU, 2, TB, CH), BF16),
             vmem((2, NJ, TOK, CH), BF16),
             vmem((NJ, 2, 2, TB, CH), F32),
-            vmem((HID, WID), F32),
-            vmem((2, 2, OWN, WID), BF16),
-            vmem((2, 2, OWN, WID), BF16),
-            vmem((2, OWN, WID), BF16),
-            vmem((2, OWN, WID), BF16),
+            vmem((NJ, CH, WID), F32),
+            vmem((NJ, 2, 2, OH, WID), BF16),
+            vmem((NJ, 2, 2, OH, WID), BF16),
+            vmem((NJ, 2, OH, WID), BF16),
+            vmem((NJ, 2, OH, WID), BF16),
             vmem((NJ, WID, CH), F32),
             vmem((NJ - 1, 2, 2, WB, CH), BF16),
             vmem((NJ - 1, 2, 2, WB, CH), BF16),
@@ -520,10 +556,10 @@
             vmem((ND, TB, DC), BF16),
             vmem((ND, TB, DC), BF16),
             vmem((TB, WID), BF16),
-            vmem((WB, WID), BF16),
+            vmem((2, WB, HID), BF16),
             vmem((WB, WID), BF16),
             dma((6,)),
-            dma((3,)),
+            dma((4,)),
             dma((15,)),
             dma((2,)),
             dma((2, 2, 3)),
@@ -531,14 +567,14 @@
             dma((NJ,)),
             dma((NJ,)),
             dma((NJ, 2)),
-            dma,
-            dma((2,)),
+            dma((NJ,)),
+            dma((NJ, 2)),
             dma((2 * NU, 2)),
             dma((2 * NU, 2)),
             dma((2 * NU, 2)),
             dma((2 * NU, 2)),
-            dma((2,)),
-            dma((2,)),
+            dma((NJ, 2)),
+            dma((NJ, 2)),
             dma((NJ - 1, 2)),
             dma((NJ - 1, 2)),
             dma((2,)),
@@ -553,7 +589,11 @@
         cost_estimate=pl.CostEstimate(flops=11 * 10**9, bytes_accessed=3 * 10**6, transcendentals=0),
     )(tokens, cotangent, weight_in, weight_out)
     return pl.pallas_call(
-        hand_over, out_shape=shapes, in_specs=[hbm] * 3, out_specs=(hbm,) * 3, scratch_shapes=[dma((3,))]
+        hand_over,
+        out_shape=shapes,
+        in_specs=[hbm] * 3,
+        out_specs=(hbm,) * 3,
+        scratch_shapes=[vmem(a.shape, BF16) for a in shapes] + [dma((6,))],
     )(*results)
 
 

time: 182 us -> 134 us (0.74)
  Pallas kernels: 181 us -> 132 us
    pallas_call x1, Pallas kernels: 41.3 us -> 2.21 us  [shards(): pl.pallas_call(hand_over, out_shape=shapes, in_specs=[hbm] * 3, out_specs...]
    pallas_call x1, Pallas kernels: 140 us -> 130 us  [shards(): pl.pallas_call(functools.partial(kernel, scale), out_shape=shapes, in_spe...]
where the time goes in v4:
time: 134 us; the launch traced here: 133 us
  Pallas kernels  132 us (99%)
    pallas_call x1, Pallas kernels, shards(): pl.pallas_call(functools.partial(kernel, scale), out_shape=shapes, in_spe...  130 us

profile of v4, /device:TPU:2, one launch (start us, length us, event | category | flops | bytes accessed | tf_op | source)
XLA Modules:
  0.0 132.9 jit_solution(9640368462784851419)
XLA Ops:
  0.6 129.9 %shard_map.67 = (bf16[48,1536]{1,0:T(8,128)(2,1)}, bf16[192,1536]{1,0:T(8,128)(2,1)}, bf16[192,1536]{1,0:T(8,128)(2,1)}) custom-call(bf16[48,1536]{1,0:T(8,128)(2,1)} %tok.1, bf16[48,1536]{1,0:T(8,128)(2,1)} %cot.1, bf16[192,1536]{1,0:T(8,128)(2,1)} %win.1, bf16[192,1536]{1,0:T(8,128)(2,1)} %wout.1), custom_call_target="tpu_custom_call" | custom-call | flops 11000000512 | bytes 3000000 | tf_op jit(solution)/shard_map/pallas_call | solution.py:518
  130.5 2.2 %shard_map.68 = (bf16[48,1536]{1,0:T(8,128)(2,1)}, bf16[192,1536]{1,0:T(8,128)(2,1)}, bf16[192,1536]{1,0:T(8,128)(2,1)}) custom-call(bf16[48,1536]{1,0:T(8,128)(2,1)} %get-tuple-element.6.refs_0_, bf16[192,1536]{1,0:T(8,128)(2,1)} %get-tuple-element.7.refs_1_, bf16[192,1536]{1,0:T(8,128)(2,1)} %get-tuple-element.8.refs_2_), custom_call_target="tpu_custom_call" | custom-call | tf_op jit(solution)/shard_map/pallas_call | solution.py:591

commit v5 on v4

--- a/solution.py
+++ b/solution.py
@@ -11,8 +11,8 @@
 BF16, F32 = jnp.bfloat16, jnp.float32
 NJ, CH = 3, 256
 NU = 2 * NJ
-ORDER = ((0, 1), (0, 0), (1, 1), (1, 0), (2, 1), (2, 0))
-ND, DC = 2, 768
+ORDER = ((0, 1), (0, 0), (1, 1), (2, 1), (1, 0), (2, 0))
+ND, DC = 3, 512
 OB, OH = 64, 32
 STEP = (1, 3)
 TB, WB = 48, 192
@@ -31,11 +31,11 @@
 
 
 def kernel(
-    scale, tok, cot, win, wout, o_tok, o_win, o_wout,
+    scale, tok, cot, win, wout, r_tok, o_win, r_wout,
     tg, wl, wst, wi, wo, pf, s1s, s1r, s2s, s2r, hg, slope, dwof, o1s, o1r, o2s, o2r,
-    dwif, i1s, i1r, i2s, i2r, dwis, dwir, dwcs, dwcr, dxf, dxss, dxsr, dxyf, dxys, dxyr, dxcs, dxcr,
-    r_tok, r_win, r_wout, m_loc, m_res, sent, m_agc, m_agy, m_ags, m_wic, m_wix, m_wif, m_wox, m_wof, m_s1, m_s2, m_h1, m_h2,
-    m_o1, m_o2, m_i1, m_i2, m_dwi, m_dwc, m_dxs, m_dxy, m_dxc,
+    dwif, dwis, dwir, dwcs, dwcr, dxf, dxss, dxsr, dxyf, dxys, dxyr, dxcs, dxcr,
+    r_win, m_loc, m_res, sent, m_agc, m_agy, m_ags, m_wic, m_wix, m_wif, m_wox, m_wof, m_s1, m_s2, m_h1, m_h2,
+    m_o1, m_o2, m_dwi, m_dwc, m_dxs, m_dxy, m_dxc,
 ):
     k, out, dep = lax.axis_index("inp"), lax.axis_index("out"), lax.axis_index("dep")
     y, co, c, x = out // 2, out % 2, dep // 4, dep % 4
@@ -157,17 +157,11 @@
     def o2(j, r):
         return cp(o2s.at[j, r], o2r.at[j, r], 7, m_o2.at[j, r], dev(dx=STEP[r]))
 
-    def i1(j, r):
-        return cp(i1s.at[j, r], i1r.at[j, r], 12, m_i1.at[j, r], dev(dx=STEP[r]))
-
-    def i2(j, r):
-        return cp(i2s.at[j, r], i2r.at[j, r], 13, m_i2.at[j, r], dev(dx=STEP[r]))
-
-    def dwi_x(p, dx):
-        return cp(dwis.at[p, dx - 1], dwir.at[p, dx - 1], 14, m_dwi.at[p], dev(dx=dx))
-
-    def dwi_x_all(p):
-        return cp(dwir.at[p], dwir.at[p], 14, m_dwi.at[p], dev(dx=1))
+    def dwi_x(j, p, dx):
+        return cp(dwis.at[j, p, dx - 1], dwir.at[j, p, dx - 1], 12, m_dwi.at[j, p], dev(dx=dx))
+
+    def dwi_x_all(j, p):
+        return cp(dwir.at[j, p], dwir.at[j, p], 12, m_dwi.at[j, p], dev(dx=1))
 
     def dw_c(j):
         return cp(dwcs.at[j], dwcr.at[j], 8, m_dwc.at[j], dev(fc=1))
@@ -264,22 +258,10 @@
 
     def weight_in_part(j):
         weight_in_half(j, 0)
-        if j == NJ - 1:
-            for p in (1, 0):
-                for d in (2, 1, 3):
-                    dwis[p, d - 1] = weight_in_piece(j, p, x + d).astype(BF16)
-                    dwi_x(p, d).start()
-        else:
-            for r in range(2):
-                i1s[j, r, 0] = weight_in_piece(j, 1 - r, x + 2).astype(BF16)
-                i1s[j, r, 1] = weight_in_piece(j, r, x + STEP[r]).astype(BF16)
-                i1(j, r).start()
-
-    def weight_in_middle(j):
-        for r in range(2):
-            i1(j, r).wait_recv()
-            i2s[j, r] = (weight_in_piece(j, 1 - r, x + STEP[r]) + i1r[j, r, 0].astype(F32)).astype(BF16)
-            i2(j, r).start()
+        for p in (1, 0):
+            for d in (2, 1, 3):
+                dwis[j, p, d - 1] = weight_in_piece(j, p, x + d).astype(BF16)
+                dwi_x(j, p, d).start()
 
     def weight_in_result(cc, j, value):
         for xx in range(4):
@@ -287,13 +269,9 @@
 
     def weight_in_sum(j, p):
         value = weight_in_piece(j, p, x)
-        if j == NJ - 1:
-            dwi_x_all(p).wait_recv()
-            for d in range(3):
-                value = value + dwir[p, d].astype(F32)
-        else:
-            i2(j, 1 - p).wait_recv()
-            value = value + i2r[j, 1 - p].astype(F32) + i1r[j, p, 1].astype(F32)
+        dwi_x_all(j, p).wait_recv()
+        for d in range(3):
+            value = value + dwir[j, p, d].astype(F32)
         if p:
             dwcs[j] = value.astype(BF16)
             dw_c(j).start()
@@ -342,9 +320,7 @@
     local = [pltpu.make_async_copy((tok, cot)[a], tslot(a, c, y, co), m_loc.at[a]) for a in range(2)]
     local += [pltpu.make_async_copy(wout.at[pl.ds(j * OB, OB)], wo.at[j, rows(x * OB, OB)], m_loc.at[2 + j]) for j in range(NJ)]
     columns = pltpu.make_async_copy(win, wl, m_loc.at[5])
-    result_tok = pltpu.make_async_copy(r_tok, o_tok, m_res.at[0])
-    result_out = pltpu.make_async_copy(r_wout, o_wout, m_res.at[1])
-    result_in = [pltpu.make_async_copy(r_win.at[i], o_win.at[:, pl.ds(i * HID, HID)], m_res.at[2 + i]) for i in range(2)]
+    result_in = [pltpu.make_async_copy(r_win.at[i], o_win.at[:, pl.ds(i * HID, HID)], m_res.at[i]) for i in range(2)]
     columns.start()
     for copy in local:
         copy.start()
@@ -424,8 +400,9 @@
         if t == NU - 1:
             for p in (0, 1):
                 ag_s_all(1, p).wait_recv()
-        if t >= NU - 1 and (t + 1 - NU) % 2 == 0 and t + 1 < 2 * NU:
-            wo_all((t + 1 - NU) // 2).wait_recv()
+        for j in range(NJ):
+            if t + 1 == NU + (0, 2, 3)[j]:
+                wo_all(j).wait_recv()
         if t + 1 < 2 * NU:
             product(t + 1)
         if t == 1:
@@ -451,12 +428,7 @@
                 weight_out_middle(j)
             if t == 2 * j + 8:
                 weight_out_finish(j)
-        if t == 2 * NU:
-            result_out.start()
         u = t - 4
-        if u == NU + 5:
-            for d in range(ND):
-                tokens_middle(1, d)
         if u >= NU:
             a, j, p = unit(u)
             arrived(u)
@@ -466,21 +438,20 @@
                 tokens_part(p, j, d)
             if not p:
                 weight_in_part(j)
-            if u == NU + 2:
-                weight_in_middle(0)
+            if u == NU + 4:
+                for d in range(ND):
+                    tokens_middle(1, d)
     for d in range(ND):
         tokens_middle(0, d)
-    weight_in_middle(1)
-    for p in (1, 0):
-        weight_in_sum(0, p)
+    weight_in_sum(0, 1)
+    weight_in_sum(0, 0)
     for d in range(ND):
         tokens_sum(1, d)
+    weight_in_sum(1, 1)
+    weight_in_sum(1, 0)
     weight_in_sum(2, 1)
-    for p in (1, 0):
-        weight_in_sum(1, p)
     for d in range(ND):
         tokens_sum(0, d)
-    result_tok.start()
     weight_in_sum(2, 0)
     for j in range(NJ):
         weight_in_finish(j)
@@ -489,24 +460,11 @@
 
     whole = (
         tg.at[:, pl.ds(0, 15 * TB)], wi.at[:, pl.ds(0, 7 * WB)], wo.at[:, pl.ds(0, 3 * OB)], s1s, s2s,
-        hg.at[:, :, pl.ds(0, 6 * OWN)], o1s, o2s, dwcs, dxss, dxyr, dxcs, i1s, i2s, dwis,
+        hg.at[:, :, pl.ds(0, 6 * OWN)], o1s, o2s, dwcs, dxss, dxyr, dxcs, dwis,
     )
     for family, ref in enumerate(whole):
         cp(ref, ref, family, m_agc.at[0], dev(fs=1)).wait_send()
-    for copy in (result_tok, result_out, *result_in):
-        copy.wait()
-
-
-def hand_over(*refs):
-    sems = refs[9]
-    loads = [pltpu.make_async_copy(refs[i], refs[6 + i], sems.at[i]) for i in range(3)]
-    stores = [pltpu.make_async_copy(refs[6 + i], refs[3 + i], sems.at[3 + i]) for i in range(3)]
-    for copy in loads:
-        copy.start()
-    for load, store in zip(loads, stores):
-        load.wait()
-        store.start()
-    for copy in stores:
+    for copy in result_in:
         copy.wait()
 
 
@@ -514,12 +472,13 @@
     scale = float(tokens.shape[0] * lax.axis_size("out") * lax.axis_size("dep")) ** (-0.5)
     vmem, dma = pltpu.VMEM, pltpu.SemaphoreType.DMA
     hbm = pl.BlockSpec(memory_space=pl.ANY)
-    shapes = tuple(jax.ShapeDtypeStruct(a.shape, BF16) for a in (tokens, weight_in, weight_out))
-    results = pl.pallas_call(
+    own = pl.BlockSpec(memory_space=pltpu.VMEM)
+    shapes = tuple(vmem(a.shape, BF16) for a in (tokens, weight_in, weight_out))
+    return pl.pallas_call(
         functools.partial(kernel, scale),
         out_shape=shapes,
         in_specs=[hbm] * 4,
-        out_specs=(hbm,) * 3,
+        out_specs=(own,) * 3,
         scratch_shapes=[
             vmem((2, TOK, WID), BF16),
             vmem((WB, 2 * HID), BF16),
@@ -539,12 +498,8 @@
             vmem((NJ, 2, OH, WID), BF16),
             vmem((NJ, 2, OH, WID), BF16),
             vmem((NJ, WID, CH), F32),
-            vmem((NJ - 1, 2, 2, WB, CH), BF16),
-            vmem((NJ - 1, 2, 2, WB, CH), BF16),
-            vmem((NJ - 1, 2, WB, CH), BF16),
-            vmem((NJ - 1, 2, WB, CH), BF16),
-            vmem((2, 3, WB, CH), BF16),
-            vmem((2, 3, WB, CH), BF16),
+            vmem((NJ, 2, 3, WB, CH), BF16),
+            vmem((NJ, 2, 3, WB, CH), BF16),
             vmem((NJ, WB, CH), BF16),
             vmem((NJ, WB, CH), BF16),
             vmem((2, ND, HALF, DC), F32),
@@ -555,11 +510,9 @@
             vmem((2, ND, 3, TB, DC), BF16),
             vmem((ND, TB, DC), BF16),
             vmem((ND, TB, DC), BF16),
-            vmem((TB, WID), BF16),
             vmem((2, WB, HID), BF16),
-            vmem((WB, WID), BF16),
             dma((6,)),
-            dma((4,)),
+            dma((2,)),
             dma((15,)),
             dma((2,)),
             dma((2, 2, 3)),
@@ -575,9 +528,7 @@
             dma((2 * NU, 2)),
             dma((NJ, 2)),
             dma((NJ, 2)),
-            dma((NJ - 1, 2)),
-            dma((NJ - 1, 2)),
-            dma((2,)),
+            dma((NJ, 2)),
             dma((NJ,)),
             dma((2, ND)),
             dma((2, ND)),
@@ -588,13 +539,6 @@
         ),
         cost_estimate=pl.CostEstimate(flops=11 * 10**9, bytes_accessed=3 * 10**6, transcendentals=0),
     )(tokens, cotangent, weight_in, weight_out)
-    return pl.pallas_call(
-        hand_over,
-        out_shape=shapes,
-        in_specs=[hbm] * 3,
-        out_specs=(hbm,) * 3,
-        scratch_shapes=[vmem(a.shape, BF16) for a in shapes] + [dma((6,))],
-    )(*results)
 
 
 def solution(mesh):

time: 134 us -> 130 us (0.970)
  Pallas kernels: 132 us -> 125 us
  local copies, waits for them, and re-layouts: 0 us -> 2.29 us
    pallas_call x1, Pallas kernels: 130 us -> 125 us  [shards(): pl.pallas_call(functools.partial(kernel, scale), out_shape=shapes, in_spe...]
    unnamed x0 -> x3, local copies, waits for them, and re-layouts: none -> 2.29 us
    pallas_call x1 -> x0, Pallas kernels: 2.21 us -> none  [shards(): pl.pallas_call(hand_over, out_shape=shapes, in_specs=[hbm] * 3, out_specs...]
where the time goes in v5:
time: 130 us; the launch traced here: 128 us
  Pallas kernels  125 us (96%)
  local copies, waits for them, and re-layouts  2.29 us (2%)
    pallas_call x1, Pallas kernels, shards(): pl.pallas_call(functools.partial(kernel, scale), out_shape=shapes, in_spe...  125 us

profile of v5, /device:TPU:2, one launch (start us, length us, event | category | flops | bytes accessed | tf_op | source)
XLA Modules:
  0.0 128.2 jit_solution(13073875190421602381)
XLA Ops:
  0.6 125.3 %shard_map.67 = (bf16[48,1536]{1,0:T(8,128)(2,1)S(1)}, bf16[192,1536]{1,0:T(8,128)(2,1)S(1)}, bf16[192,1536]{1,0:T(8,128)(2,1)S(1)}) custom-call(bf16[48,1536]{1,0:T(8,128)(2,1)} %tok.1, bf16[48,1536]{1,0:T(8,128)(2,1)} %cot.1, bf16[192,1536]{1,0:T(8,128)(2,1)} %win.1, bf16[192,1536]{1,0:T(8,128)(2,1)} %wout.1), custom_call_target="tpu_custom_call" | custom-call | flops 11000000512 | bytes 3000000 | tf_op jit(solution)/shard_map/pallas_call | solution.py:477
  125.9 0.7 copy.10
  126.6 0.8 copy.11
  127.4 0.8 copy.12

commit v6 on v5

--- a/solution.py
+++ b/solution.py
@@ -134,22 +134,36 @@
         return (a, *ORDER[i]) if a else (a, i // 2, i % 2)
 
     def s1(u, r):
-        return cp(s1s.at[u, r], s1r.at[u, r], 3, m_s1.at[u, r], dev(dk=STEP[r]))
+        return cp(s1s.at[u, r, 0], s1r.at[u, r, 0], 3, m_s1.at[u, r], dev(dk=STEP[r]))
+
+    def s1_own(u, r):
+        return cp(s1s.at[u, r, 1], s1r.at[u, r, 1], 3, m_s2.at[u], dev(dk=STEP[r]))
 
     def s2(u, r):
-        return cp(s2s.at[u, r], s2r.at[u, r], 4, m_s2.at[u, r], dev(dk=STEP[r]))
+        return cp(s2s.at[u, r], s2r.at[u, r], 4, m_s2.at[u], dev(dk=STEP[r]))
+
+    def s2_all(u):
+        return cp(s1r.at[u], s1r.at[u], 4, m_s2.at[u], dev(dk=1))
 
     def hrows(u, owner, part, n):
         a, j, p = unit(u)
         return hg.at[a, j, rows(half[p] * HALF + owner % 4 * OWN + part * TB, n)]
 
     def h1(u, r):
-        slot = hrows(u, k, 0, OWN)
+        slot = hrows(u, k, r, TB)
         return cp(slot, slot, 5, m_h1.at[u, r], dev(dk=STEP[r]))
+
+    def h1_own(u, r):
+        slot = hrows(u, k, 1 - r, TB)
+        return cp(slot, slot, 5, m_h2.at[u], dev(dk=STEP[r]))
 
     def h2(u, r):
         slot = hrows(u, k + STEP[1 - r], r, TB)
-        return cp(slot, slot, 5, m_h2.at[u, r], dev(dk=STEP[r]))
+        return cp(slot, slot, 5, m_h2.at[u], dev(dk=STEP[r]))
+
+    def h2_all(u):
+        ref = hg.at[0, 0, pl.ds(0, 4 * TB)]
+        return cp(ref, ref, 5, m_h2.at[u], dev(dk=1))
 
     def o1(j, r):
         return cp(o1s.at[j, r], o1r.at[j, r], 6, m_o1.at[j, r], dev(dx=STEP[r]))
@@ -186,12 +200,12 @@
         def piece(owner, part):
             return pf[u % 4, rows(owner % 4 * OWN + part * TB, TB)].astype(BF16)
 
-        s1s[u, 0, 0] = piece(k + 2, 0)
-        s1s[u, 0, 1] = piece(k + 1, 1)
-        s1(u, 0).start()
-        s1s[u, 1, 0] = piece(k + 2, 1)
-        s1s[u, 1, 1] = piece(k + 3, 0)
-        s1(u, 1).start()
+        for r in range(2):
+            s1s[u, r, 0] = piece(k + 2, r)
+            s1(u, r).start()
+        for r in range(2):
+            s1s[u, r, 1] = piece(k + STEP[r], 1 - r)
+            s1_own(u, r).start()
 
     def middle(u):
         for r in range(2):
@@ -202,8 +216,8 @@
 
     def finish(u):
         a, j, p = unit(u)
-        for r in range(2):
-            s2(u, r).wait_recv()
+        s2_all(u).wait_recv()
+        for r in range(2):
             value = pf[u % 4, rows(k * OWN + r * TB, TB)] + s2r[u, r].astype(F32) + s1r[u, 1 - r, 1].astype(F32)
             if a:
                 value = value * slope[j, p, r]
@@ -213,14 +227,17 @@
         for r in range(2):
             h1(u, r).start()
 
+    def finish_sent(u):
+        for r in range(2):
+            h1_own(u, r).start()
+
     def forward(u):
         for r in range(2):
             h1(u, r).wait_recv()
             h2(u, r).start()
 
     def arrived(u):
-        for r in range(2):
-            h2(u, r).wait_recv()
+        h2_all(u).wait_recv()
 
     def weight_out_part(j):
         dwof[j] = scale * dot(hg[0, j], tg[1], 0, 0)
@@ -405,6 +422,8 @@
                 wo_all(j).wait_recv()
         if t + 1 < 2 * NU:
             product(t + 1)
+        if 0 <= t - 2 < 2 * NU:
+            finish_sent(t - 2)
         if t == 1:
             wo_send(0)
         if t == 2:
@@ -523,9 +542,9 @@
             dma((NJ,)),
             dma((NJ, 2)),
             dma((2 * NU, 2)),
+            dma((2 * NU,)),
             dma((2 * NU, 2)),
-            dma((2 * NU, 2)),
-            dma((2 * NU, 2)),
+            dma((2 * NU,)),
             dma((NJ, 2)),
             dma((NJ, 2)),
             dma((NJ, 2)),

time: 130 us -> 129 us (level)
    pallas_call x1, Pallas kernels: 125 us -> 124 us  [shards(): pl.pallas_call(functools.partial(kernel, scale), out_shape=shapes, in_spe...]
where the time goes in v6:
time: 129 us; the launch traced here: 126 us
  Pallas kernels  124 us (96%)
  local copies, waits for them, and re-layouts  2.29 us (2%)
    pallas_call x1, Pallas kernels, shards(): pl.pallas_call(functools.partial(kernel, scale), out_shape=shapes, in_spe...  124 us

profile of v6, /device:TPU:2, one launch (start us, length us, event | category | flops | bytes accessed | tf_op | source)
XLA Modules:
  0.0 126.5 jit_solution(12637514693098135078)
XLA Ops:
  0.6 123.5 %shard_map.67 = (bf16[48,1536]{1,0:T(8,128)(2,1)S(1)}, bf16[192,1536]{1,0:T(8,128)(2,1)S(1)}, bf16[192,1536]{1,0:T(8,128)(2,1)S(1)}) custom-call(bf16[48,1536]{1,0:T(8,128)(2,1)} %tok.1, bf16[48,1536]{1,0:T(8,128)(2,1)} %cot.1, bf16[192,1536]{1,0:T(8,128)(2,1)} %win.1, bf16[192,1536]{1,0:T(8,128)(2,1)} %wout.1), custom_call_target="tpu_custom_call" | custom-call | flops 11000000512 | bytes 3000000 | tf_op jit(solution)/shard_map/pallas_call | solution.py:496
  124.2 0.7 copy.10
  124.8 0.8 copy.11
  125.7 0.8 copy.12

commit v7 on v6

--- a/solution.py
+++ b/solution.py
@@ -166,10 +166,16 @@
         return cp(ref, ref, 5, m_h2.at[u], dev(dk=1))
 
     def o1(j, r):
-        return cp(o1s.at[j, r], o1r.at[j, r], 6, m_o1.at[j, r], dev(dx=STEP[r]))
+        return cp(o1s.at[j, r, 0], o1r.at[j, r, 0], 6, m_o1.at[j, r], dev(dx=STEP[r]))
+
+    def o1_own(j, r):
+        return cp(o1s.at[j, r, 1], o1r.at[j, r, 1], 6, m_o2.at[j], dev(dx=STEP[r]))
 
     def o2(j, r):
-        return cp(o2s.at[j, r], o2r.at[j, r], 7, m_o2.at[j, r], dev(dx=STEP[r]))
+        return cp(o2s.at[j, r], o2r.at[j, r], 7, m_o2.at[j], dev(dx=STEP[r]))
+
+    def o2_all(j):
+        return cp(o1r.at[j], o1r.at[j], 7, m_o2.at[j], dev(dx=1))
 
     def dwi_x(j, p, dx):
         return cp(dwis.at[j, p, dx - 1], dwir.at[j, p, dx - 1], 12, m_dwi.at[j, p], dev(dx=dx))
@@ -247,8 +253,10 @@
 
         for r in range(2):
             o1s[j, r, 0] = piece(x + 2, r)
+            o1(j, r).start()
+        for r in range(2):
             o1s[j, r, 1] = piece(x + STEP[r], 1 - r)
-            o1(j, r).start()
+            o1_own(j, r).start()
 
     def weight_out_middle(j):
         for r in range(2):
@@ -258,8 +266,8 @@
             o2(j, r).start()
 
     def weight_out_finish(j):
-        for r in range(2):
-            o2(j, r).wait_recv()
+        o2_all(j).wait_recv()
+        for r in range(2):
             value = dwof[j, rows(x * OB + r * OH, OH)] + o2r[j, r].astype(F32) + o1r[j, 1 - r, 1].astype(F32)
             r_wout[pl.ds(j * OB + r * OH, OH)] = value.astype(BF16)
 
@@ -546,7 +554,7 @@
             dma((2 * NU, 2)),
             dma((2 * NU,)),
             dma((NJ, 2)),
-            dma((NJ, 2)),
+            dma((NJ,)),
             dma((NJ, 2)),
             dma((NJ,)),
             dma((2, ND)),

time: 129 us -> 128 us (level)
  no operation moved by 1% of the time
where the time goes in v7:
time: 128 us; the launch traced here: 126 us
  Pallas kernels  123 us (96%)
  local copies, waits for them, and re-layouts  2.29 us (2%)
    pallas_call x1, Pallas kernels, shards(): pl.pallas_call(functools.partial(kernel, scale), out_shape=shapes, in_spe...  123 us

profile of v7, /device:TPU:2, one launch (start us, length us, event | category | flops | bytes accessed | tf_op | source)
XLA Modules:
  0.0 126.0 jit_solution(13842382077748360790)
XLA Ops:
  0.6 123.1 %shard_map.67 = (bf16[48,1536]{1,0:T(8,128)(2,1)S(1)}, bf16[192,1536]{1,0:T(8,128)(2,1)S(1)}, bf16[192,1536]{1,0:T(8,128)(2,1)S(1)}) custom-call(bf16[48,1536]{1,0:T(8,128)(2,1)} %tok.1, bf16[48,1536]{1,0:T(8,128)(2,1)} %cot.1, bf16[192,1536]{1,0:T(8,128)(2,1)} %win.1, bf16[192,1536]{1,0:T(8,128)(2,1)} %wout.1), custom_call_target="tpu_custom_call" | custom-call | flops 11000000512 | bytes 3000000 | tf_op jit(solution)/shard_map/pallas_call | solution.py:504
  123.7 0.7 copy.10
  124.4 0.8 copy.11
  125.2 0.8 copy.12
